TPU v7x, 256 devices: a whole 4x4x8 slice. The times are simulated.
256 devices in a mesh: dp: 16 (over y, z_hi), tensor: 16 (over x, z_lo, core).
Axes of the slice: x: 4, y: 4, z: 8 (z_hi: 4, z_lo: 2; z = z_hi * 2 + z_lo), core: 2. Of those that a mesh axis runs over, the one named last changes fastest.
Arguments:
- attention_output: bfloat16 [8192, 8192], P('dp', 'tensor'), may hold values from -6 to 6
- frozen_weight: bfloat16 [8192, 8192], P('tensor'), may hold values from -0.0625 to 0.0625
- output_gradient: bfloat16 [8192, 8192], P('dp', 'tensor'), may hold values from -6 to 6
- tenant_token_count: int32 [16, 64], P('dp'), may hold values from 1 to 256, 512 in all within a row
- tenant_storage_slot: int32 [64], replicated, may hold values from 0 to 63, each once
- adapter_down_weight: float32 [64, 8192, 16], P('dp', 'tensor'), may hold values from -0.0625 to 0.0625
- adapter_up_weight: float32 [64, 16, 8192], P('dp', None, 'tensor'), may hold values from -1.5 to 1.5
- down_first_moment: float32 [64, 8192, 16], P('dp', 'tensor'), may hold values from -60 to 60
- down_second_moment: float32 [64, 8192, 16], P('dp', 'tensor'), may hold values from 1 to 10000
- up_first_moment: float32 [64, 16, 8192], P('dp', None, 'tensor'), may hold values from -60 to 60
- up_second_moment: float32 [64, 16, 8192], P('dp', None, 'tensor'), may hold values from 1 to 10000
Outputs:
- proj_out: bfloat16 [8192, 8192], P('dp', 'tensor')
- input_grad: bfloat16 [8192, 8192], P('dp', 'tensor')
- updated_down_weight: float32 [64, 8192, 16], P('dp', 'tensor')
- updated_up_weight: float32 [64, 16, 8192], P('dp', None, 'tensor')
- updated_down_first_moment: float32 [64, 8192, 16], P('dp', 'tensor')
- updated_down_second_moment: float32 [64, 8192, 16], P('dp', 'tensor')
- updated_up_first_moment: float32 [64, 16, 8192], P('dp', None, 'tensor')
- updated_up_second_moment: float32 [64, 16, 8192], P('dp', None, 'tensor')
Inputs may be any that keep to these rules, and one draw needn't show every extreme that they name: `tenant_token_count`: each row sums to 512; every tenant has at least one token in every row; tokens of one dp index are sorted by tenant. `tenant_storage_slot`: a permutation of the slots.
All inputs are finite; a program needn't handle non-finite values.
Results may differ from a plain program's by a relative error of at most 0.02.
Values may be sent and summed in bfloat16 or wider, within the bound.
No kernel may reach another device: no remote copies, remote signals or barrier semaphores. Data moves between devices by JAX's collectives and lax.ppermute only.
A program may use at most 128 MiB of HBM per device.

v0:
```python
import functools

import jax
import jax.numpy as jnp
from jax import lax
from jax.experimental import pallas as pl
from jax.experimental.pallas import tpu as pltpu
from jax.sharding import Mesh
from jax.sharding import PartitionSpec as P

DP = ("y", "zh")
TENSOR = ("x", "zl", "c")
BF = jnp.bfloat16
F32 = jnp.float32
RING = (0, 3, 1, 2)
VMEM_LIMIT = 16 * 1024 * 1024
WEIGHT_LIMIT = 46 * 1024 * 1024


def send(a, axis, step):
    n = lax.axis_size(axis)
    return lax.ppermute(a, axis, [(i, (i + step) % n) for i in range(n)])


def nn(a, b):
    return lax.dot_general(a, b, (((1,), (0,)), ((), ())), preferred_element_type=F32)


def nt(a, b):
    return lax.dot_general(a, b, (((1,), (1,)), ((), ())), preferred_element_type=F32)


def tn(a, b):
    return lax.dot_general(a, b, (((0,), (0,)), ((), ())), preferred_element_type=F32)


def call(body, out, ins, flops=0):
    size = sum(a.size * a.dtype.itemsize for a in ins) + sum(o.size * o.dtype.itemsize for o in out)
    return pl.pallas_call(
        body,
        out_shape=out,
        in_specs=[pl.BlockSpec(memory_space=pltpu.VMEM)] * len(ins),
        out_specs=[pl.BlockSpec(memory_space=pltpu.VMEM)] * len(out),
        compiler_params=pltpu.CompilerParams(vmem_limit_bytes=VMEM_LIMIT),
        cost_estimate=pl.CostEstimate(flops=flops, bytes_accessed=size, transcendentals=0),
    )(*ins)


def shape(rows, cols, dtype):
    return jax.ShapeDtypeStruct((rows, cols), dtype)


def mask_body(rank, per, slots_ref, counts_ref, place_ref, out_ref):
    rows, toks = out_ref.shape
    tenants = slots_ref.shape[1]
    row = lax.broadcasted_iota(jnp.int32, (rows, 1), 0)
    block = row // (rank * per)
    y = block // 4
    z = block - 4 * y
    ring_y = jnp.where(y == 1, 3, jnp.where(y == 2, 1, jnp.where(y == 3, 2, 0)))
    ring_z = jnp.where(z == 1, 3, jnp.where(z == 2, 1, jnp.where(z == 3, 2, 0)))
    at = ((place_ref[0] + ring_y) % 4) * 4 + (place_ref[1] + ring_z) % 4
    slot = at * per + (row // rank) % per
    lane = lax.broadcasted_iota(jnp.int32, (rows, tenants), 1).astype(F32)
    counts = counts_ref[...].astype(F32)
    hit = jnp.where(slots_ref[...] == slot, 1.0, 0.0)
    tenant = jnp.sum(hit * lane, axis=1, keepdims=True)
    first = jnp.sum(jnp.where(lane < tenant, counts, 0.0), axis=1, keepdims=True)
    last = first + jnp.sum(hit * counts, axis=1, keepdims=True)
    tok = lax.broadcasted_iota(jnp.int32, (1, toks), 1).astype(F32)
    for r in range(0, rows, 256):
        inside = (tok >= first[r : r + 256]) & (tok < last[r : r + 256])
        out_ref[r : r + 256] = jnp.where(inside, 1.0, 0.0).astype(BF)


def token_mask(slots, counts, place, rank, per, toks):
    rows = slots.shape[0] * rank
    return pl.pallas_call(
        functools.partial(mask_body, rank, per),
        out_shape=shape(rows, toks, BF),
        in_specs=[
            pl.BlockSpec(memory_space=pltpu.VMEM),
            pl.BlockSpec(memory_space=pltpu.VMEM),
            pl.BlockSpec(memory_space=pltpu.SMEM),
        ],
        out_specs=pl.BlockSpec(memory_space=pltpu.VMEM),
        compiler_params=pltpu.CompilerParams(vmem_limit_bytes=VMEM_LIMIT),
        cost_estimate=pl.CostEstimate(flops=0, bytes_accessed=rows * toks * 4, transcendentals=0),
    )(slots.reshape(1, -1), counts, place)


def narrow_body(rank, x_ref, dy_ref, m_ref, own_ref, left_ref, right_ref, far_d_ref, far_u_ref, out_ref):
    n = far_d_ref.shape[0]
    x, dy = x_ref[...], dy_ref[...]
    downs = [own_ref[:n], left_ref[:n], right_ref[:n], far_d_ref[...]]
    ups = [own_ref[n:], left_ref[n:], right_ref[n:], far_u_ref[...]]
    for k, (side, blocks) in enumerate(((x, downs), (dy, ups))):
        total = None
        for g, block in enumerate(blocks):
            wide = nt(block, side) * m_ref[g * n : (g + 1) * n].astype(F32)
            part = jnp.sum(wide.reshape(n // rank, rank, wide.shape[1]), axis=0)
            total = part if total is None else total + part
        out_ref[k * rank : (k + 1) * rank] = total


def widen(lb_ref, m_ref, g, n, which, rank):
    narrow = lb_ref[which * rank : (which + 1) * rank].astype(BF)
    return jnp.concatenate([narrow] * (n // rank), axis=0) * m_ref[g * n : (g + 1) * n]


def grad_far_body(rank, x_ref, dy_ref, m_ref, lb_ref, down_ref, up_ref):
    n = down_ref.shape[0]
    down_ref[...] = (2.0 * nn(widen(lb_ref, m_ref, 3, n, 1, rank), x_ref[...])).astype(BF)
    up_ref[...] = (2.0 * nn(widen(lb_ref, m_ref, 3, n, 0, rank), dy_ref[...])).astype(BF)


def grad_near_body(rank, x_ref, dy_ref, m_ref, lb_ref, got_down_ref, got_up_ref, left_ref, right_ref):
    n = got_down_ref.shape[0]
    x, dy = x_ref[...], dy_ref[...]
    left_ref[:n] = (2.0 * nn(widen(lb_ref, m_ref, 1, n, 1, rank), x)).astype(BF)
    left_ref[n:] = (
        2.0 * nn(widen(lb_ref, m_ref, 1, n, 0, rank), dy) + got_up_ref[...].astype(F32)
    ).astype(BF)
    right_ref[:n] = (
        2.0 * nn(widen(lb_ref, m_ref, 2, n, 1, rank), x) + got_down_ref[...].astype(F32)
    ).astype(BF)
    right_ref[n:] = (2.0 * nn(widen(lb_ref, m_ref, 2, n, 0, rank), dy)).astype(BF)


def grad_own_body(
    rank, x_ref, dy_ref, m_ref, lb_ref, a_ref, b_ref, far_ref, left_ref, right_ref, own_ref
):
    n = a_ref.shape[0] // 2
    q = n // 4
    for k, side in ((0, x_ref), (1, dy_ref)):
        rows = slice(k * n, (k + 1) * n)
        total = 2.0 * nn(widen(lb_ref, m_ref, 0, n, 1 - k, rank), side[...])
        total = total + a_ref[rows].astype(F32) + b_ref[rows].astype(F32)
        own_ref[k * q : (k + 1) * q] = total[:q]
        for i, ref in enumerate((left_ref, right_ref, far_ref)):
            ref[k * q : (k + 1) * q] = total[(i + 1) * q : (i + 2) * q].astype(BF)


def back_body(rank, get, ins, outs):
    x, x2, m_ref, lb_ref, own_ref, left_ref, right_ref, far_d_ref, far_u_ref, *parts = ins
    lifted, own_out, other_out = outs
    n = far_d_ref.shape[0]
    rows = x.shape[0]
    downs = [own_ref[:n], left_ref[:n], right_ref[:n], far_d_ref[...]]
    ups = [own_ref[n:], left_ref[n:], right_ref[n:], far_u_ref[...]]
    total = [None, None]
    for which, blocks in ((0, ups), (1, downs)):
        for g, block in enumerate(blocks):
            part = tn(widen(lb_ref, m_ref, g, n, which, rank), block)
            total[which] = part if g == 0 else total[which] + part
    w, v = get(0, 0), get(0, 1)
    lifted[...] = 2.0 * total[0] + nn(x[...], w) + nn(x2[...], v)
    first = parts[0][...]
    own = 2.0 * total[1] + nt(first, w)
    other = nt(first, v)
    for i in range(1, 8):
        part = parts[i][:rows]
        own = own + nt(part, get(i, 0))
        other = other + nt(part, get(i, 1))
    own_out[...] = own
    other_out[...] = other.astype(BF)


def with_weight(body, blocks, w, other, places, ins, out, flops):
    n = w.shape[0]
    k, m = len(blocks), len(ins)

    def run(place_ref, w_ref, v_ref, *refs):
        bufs, sems = refs[-2:]
        copies = {}
        for i, r in enumerate(blocks):
            at = pl.ds(pl.multiple_of(place_ref[r] * n, n), n)
            for j, src in enumerate((w_ref, v_ref)):
                copies[i, j] = pltpu.make_async_copy(src.at[:, at], bufs.at[i, j], sems.at[i, j])
                copies[i, j].start()

        def get(i, j):
            copies[i, j].wait()
            return bufs[i, j]

        body(get, refs[:m], refs[m:-2])

    size = 2 * k * n * n * 2 + sum(a.size * a.dtype.itemsize for a in (*ins, *out))
    return pl.pallas_call(
        run,
        in_specs=[pl.BlockSpec(memory_space=pltpu.SMEM)]
        + [pl.BlockSpec(memory_space=pltpu.HBM)] * 2
        + [pl.BlockSpec(memory_space=pltpu.VMEM)] * m,
        out_specs=[pl.BlockSpec(memory_space=pltpu.VMEM)] * len(out),
        out_shape=out,
        scratch_shapes=[pltpu.VMEM((k, 2, n, n), BF), pltpu.SemaphoreType.DMA((k, 2))],
        compiler_params=pltpu.CompilerParams(vmem_limit_bytes=WEIGHT_LIMIT),
        cost_estimate=pl.CostEstimate(flops=flops, bytes_accessed=size, transcendentals=0),
    )(places, w, other, *ins)


def two(x_ref, x2_ref, get, i):
    return nn(x_ref[...], get(i, 0)) + nn(x2_ref[...], get(i, 1))


def first_body(get, ins, outs):
    outs[0][...] = two(*ins, get, 0).astype(BF)


def far_body(get, ins, outs):
    x, x2, from_z = ins
    to_left, to_right = outs
    n = from_z.shape[0]
    h = n // 2
    far = two(x, x2, get, 0) + from_z[...].astype(F32)
    to_left[n:] = far[h:].astype(BF)
    to_right[n:] = far[:h].astype(BF)
    to_left[:n] = two(x, x2, get, 1).astype(BF)
    to_right[:n] = two(x, x2, get, 2).astype(BF)


def near_body(get, ins, outs):
    x, x2, from_left, from_right = ins
    left, right, z = outs
    n = left.shape[0]
    h = n // 2
    a = two(x, x2, get, 0)
    left[:h] = a[:h].astype(BF)
    left[h:] = (a[h:] + from_right[n:].astype(F32)).astype(BF)
    b = two(x, x2, get, 1)
    right[:h] = (b[:h] + from_left[n:].astype(F32)).astype(BF)
    right[h:] = b[h:].astype(BF)
    c = two(x, x2, get, 2)
    z[...] = (c + from_left[:n].astype(F32) + from_right[:n].astype(F32)).astype(BF)


def last_body(a, b, c, own, out):
    total = own[...] + a[...].astype(F32) + b[...].astype(F32) + c[...].astype(F32)
    out[...] = total.astype(BF)


def pack_body(z, left, right, to_left, to_right):
    n = z.shape[0]
    h = n // 2
    to_left[:n] = z[...]
    to_left[n:] = right[h:]
    to_right[:n] = z[...]
    to_right[n:] = left[:h]


def join_body(left, right, out):
    h = out.shape[0] // 2
    out[:h] = left[2 * h :]
    out[h:] = right[2 * h :]


def round_body(down, up, out):
    n = down.shape[0]
    out[:n] = down[...].astype(BF)
    out[n:] = up[...].astype(BF)


def group_body(own, left, right, far, out):
    n = own.shape[0] // 2
    for k in range(2):
        for i, a in enumerate((own, left, right, far)):
            out[(4 * k + i) * n : (4 * k + i + 1) * n] = a[k * n : (k + 1) * n]


def sum_body(a, b, out):
    out[...] = (a[...] + b[...].astype(F32)).astype(BF)


def adam_body(*refs):
    own, a, b, c = refs[:4]
    rows = own.shape[0] // 2
    ins, outs = refs[4:10], refs[10:]
    corr_one = 1.0 - 0.9**10
    corr_two = 1.0 - 0.999**10
    for k in range(2):
        at = slice(k * rows, (k + 1) * rows)
        grad = own[at] + a[at].astype(F32) + b[at].astype(F32) + c[at].astype(F32)
        param = ins[3 * k][...]
        first = 0.9 * ins[3 * k + 1][...] + 0.1 * grad
        second = 0.999 * ins[3 * k + 2][...] + 0.001 * grad * grad
        step = first / corr_one / (jnp.sqrt(second / corr_two) + 1e-08)
        outs[3 * k][...] = param - 0.01 * (step + 0.1 * param)
        outs[3 * k + 1][...] = first
        outs[3 * k + 2][...] = second


def tie(a, *before):
    return lax.optimization_barrier((a, *before))[0]


def local(x, w, dy, counts, slots, down, up, down_m, down_v, up_m, up_v):
    toks, n = x.shape
    per, rank = up.shape[0], up.shape[1]
    flat = per * rank
    n4 = 4 * flat
    half = toks // 2
    dot = 2 * toks * n * n
    block, wide = shape(toks, n, BF), shape(toks, n, F32)
    iy, iz, ix, il, ic = (lax.axis_index(a) for a in (*DP, *TENSOR))

    def down_rows(a):
        return jnp.transpose(a, (0, 2, 1)).reshape(flat, n)

    def up_rows(a):
        return a.reshape(flat, n)

    columns = [((ix + s) % 4) * 4 + ((il + t) % 2) * 2 + ic for t in (0, 1) for s in RING]
    places = jnp.stack(columns).astype(jnp.int32)

    pack = shape(toks + half, n, BF)

    def weighed(body, blocks, ins, out):
        return with_weight(body, blocks, w, other, places, ins, out, 2 * len(blocks) * dot)

    x2 = send(x, "c", 1)
    mine = call(round_body, [shape(2 * flat, n, BF)], (down_rows(down), up_rows(up)))[0]
    z_left, z_right, z_far = (send(tie(mine, x2), "zh", k) for k in (1, -1, 2))
    d_left, d_right = send(dy, "x", 1), send(dy, "x", -1)
    mask = token_mask(slots, counts, jnp.stack([iy, iz]).astype(jnp.int32), rank, per, toks)
    group = call(group_body, [shape(2 * n4, n, BF)], (tie(mine, mask), z_left, z_right, z_far))[0]
    y_left, y_right = send(group, "y", 1), send(group, "y", -1)
    other = send(tie(w, group), "c", 1)
    d_z = send(tie(dy, group), "zl", 1)
    to_left, to_right = call(pack_body, [pack] * 2, (d_z, d_left, d_right))
    y_far_d = send(y_left[:n4], "y", 1)
    y_far_u = send(y_right[n4:], "y", -1)
    a_left, a_right = send(to_right, "x", 1), send(to_left, "x", -1)
    zf = weighed(first_body, (7,), (x, x2), [block])[0]
    from_z = send(zf, "zl", 1)
    p_left, p_right = weighed(far_body, (3, 5, 6), (x, x2, from_z), [pack] * 2)
    adapters = (group, y_left, y_right, y_far_d, y_far_u)


    lb = call(
        functools.partial(narrow_body, rank),
        [shape(2 * rank, toks, F32)],
        (x, dy, tie(mask, p_left, a_left, a_right), *adapters),
        flops=4 * dot,
    )[0]
    lb = lb + send(lb, "c", 1)
    lb = lb + send(lb, "zl", 1)
    lb = lb + send(lb, "x", 1)
    lb = lb + send(lb, "x", 2)
    d_far = call(join_body, [block], (a_left, a_right))[0]

    fd, fu = call(
        functools.partial(grad_far_body, rank),
        [shape(n4, n, BF), shape(n4, n, BF)],
        (x, dy, mask, lb),
        flops=dot,
    )
    got_d, got_u = send(fd, "y", 1), send(fu, "y", -1)
    p_left, p_right, d_far_late = lax.optimization_barrier((p_left, p_right, d_far, lb))[:3]
    b_right, b_left = send(p_left, "x", -1), send(p_right, "x", 1)
    d_zf = send(d_far_late, "zl", 1)
    g_left, g_right = call(
        functools.partial(grad_near_body, rank),
        [shape(2 * n4, n, BF), shape(2 * n4, n, BF)],
        (x, dy, mask, lb, got_d, got_u),
        flops=2 * dot,
    )
    got_l, got_r = send(g_left, "y", -1), send(g_right, "y", 1)
    left, right, z = weighed(near_body, (1, 2, 4), (x, x2, tie(b_left, d_zf), b_right), [block] * 3)
    sums = (send(left, "x", -1), send(right, "x", 1), send(z, "zl", 1))
    lifted, own_grad, to_other = weighed(
        functools.partial(back_body, rank),
        tuple(range(8)),
        (
            x,
            x2,
            mask,
            lb,
            *adapters,
            tie(dy, left),
            d_left,
            d_right,
            d_far,
            d_z,
            a_left,
            a_right,
            d_zf,
        ),
        [wide, wide, block],
    )
    from_other = send(to_other, "c", 1)
    g_far, g_left, g_right, g_own = call(
        functools.partial(grad_own_body, rank),
        [shape(2 * flat, n, BF)] * 3 + [shape(2 * flat, n, F32)],
        (x, dy, mask, lb, tie(got_l, *sums, lifted), got_r),
        flops=dot,
    )
    from_far = send(g_far, "zh", 2)
    from_left, from_right = send(g_right, "zh", 1), send(g_left, "zh", -1)
    input_grad = call(sum_body, [block], (tie(own_grad, g_far), from_other))[0]

    new = call(
        adam_body,
        [shape(flat, n, F32)] * 6,
        (
            g_own,
            from_left,
            from_right,
            from_far,
            *(down_rows(a) for a in (down, down_m, down_v)),
            *(up_rows(a) for a in (up, up_m, up_v)),
        ),
    )
    new_down = [jnp.transpose(a.reshape(per, rank, n), (0, 2, 1)) for a in new[:3]]
    new_up = [a.reshape(per, rank, n) for a in new[3:]]
    proj_out = call(last_body, [block], (*sums, lifted))[0]
    return (
        proj_out,
        input_grad,
        new_down[0],
        new_up[0],
        new_down[1],
        new_down[2],
        new_up[1],
        new_up[2],
    )


def solution(mesh):
    torus = Mesh(mesh.devices.reshape(4, 4, 4, 2, 2), (*DP, *TENSOR))
    return jax.shard_map(
        local,
        mesh=torus,
        in_specs=(
            P(DP, TENSOR),
            P(TENSOR, None),
            P(DP, TENSOR),
            P(DP, None),
            P(),
            P(DP, TENSOR, None),
            P(DP, None, TENSOR),
            P(DP, TENSOR, None),
            P(DP, TENSOR, None),
            P(DP, None, TENSOR),
            P(DP, None, TENSOR),
        ),
        out_specs=(
            P(DP, TENSOR),
            P(DP, TENSOR),
            P(DP, TENSOR, None),
            P(DP, None, TENSOR),
            P(DP, TENSOR, None),
            P(DP, TENSOR, None),
            P(DP, None, TENSOR),
            P(DP, None, TENSOR),
        ),
        check_vma=False,
    )
```

profile of v0, /device:TPU:32, one launch (start us, length us, event | category | flops | bytes accessed | tf_op | source)
XLA Modules:
  0.0 144.7 jit_solution(11509458153255711079)
XLA Ops:
  2.8 3.3 %collective-permute-start.1 = (bf16[128,512]{1,0:T(8,128)(2,1)S(1)}, bf16[128,512]{1,0:T(8,128)(2,1)S(1)}, u32[]{:S(2)}, u32[]{:S(2)}) collective-permute-start(bf16[128,512]{1,0:T(8,128)(2,1)S(1)} %shard_map.170.own), channel_id=1, source_target_pairs={{0,16},{16,32},{32,48},{48,0},{1,17},{17,33},{33,49},{49,1},{2,18}... | collective-permute-start | bytes 393224 | tf_op jit(solution)/shard_map/ppermute | solution.py:22
  6.1 2.2 %collective-permute-start.2 = (bf16[128,512]{1,0:T(8,128)(2,1)S(1)}, bf16[128,512]{1,0:T(8,128)(2,1)S(1)}, u32[]{:S(2)}, u32[]{:S(2)}) collective-permute-start(bf16[128,512]{1,0:T(8,128)(2,1)S(1)} %shard_map.170.own), channel_id=1, source_target_pairs={{0,48},{16,0},{32,16},{48,32},{1,49},{17,1},{33,17},{49,33},{2,50}... | collective-permute-start | bytes 393224 | tf_op jit(solution)/shard_map/ppermute | solution.py:22
  8.3 5.0 %collective-permute-start.3 = (bf16[128,512]{1,0:T(8,128)(2,1)S(1)}, bf16[128,512]{1,0:T(8,128)(2,1)S(1)}, u32[]{:S(2)}, u32[]{:S(2)}) collective-permute-start(bf16[128,512]{1,0:T(8,128)(2,1)S(1)} %shard_map.170.own), channel_id=1, source_target_pairs={{0,32},{16,48},{32,0},{48,16},{1,33},{17,49},{33,1},{49,17},{2,34}... | collective-permute-start | bytes 393224 | tf_op jit(solution)/shard_map/ppermute | solution.py:22
  14.7 1.7 %shard_map.171.m_ref.refs_2_ = bf16[1024,512]{1,0:T(8,128)(2,1)S(1)} custom-call(s32[1,64]{1,0:T(1,128)S(1)} %bitcast.43, s32[1,64]{1,0:T(1,128)S(1)} %copy-done.21, s32[2]{0:T(128)S(1)} %pad_add_fusion.place_ref), custom_call_target="tpu_custom_call" | custom-call | bytes 2097152 | tf_op jit(solution)/shard_map/pallas_call | solution.py:78
  16.4 8.2 %collective-permute-done.3.far = bf16[128,512]{1,0:T(8,128)(2,1)S(1)} collective-permute-done((bf16[128,512]{1,0:T(8,128)(2,1)S(1)}, bf16[128,512]{1,0:T(8,128)(2,1)S(1)}, u32[]{:S(2)}, u32[]{:S(2)}) %collective-permute-start.3) | collective-permute-done | bytes 131104 | tf_op jit(solution)/shard_map/ppermute | solution.py:22
  24.7 1.6 %collective-permute-start.7 = (bf16[512,512]{1,0:T(8,128)(2,1)}, bf16[512,512]{1,0:T(8,128)(2,1)S(1)}, u32[]{:S(2)}, u32[]{:S(2)}) collective-permute-start(bf16[512,512]{1,0:T(8,128)(2,1)} %dy_ref.7), channel_id=1, source_target_pairs={{0,4},{4,8},{8,12},{12,0},{1,5},{5,9},{9,13},{13,1},{2,6},{6,10},{... | collective-permute-start | bytes 1572872 | tf_op jit(solution)/shard_map/ppermute | solution.py:22
  26.3 1.7 %collective-permute-start.8 = (bf16[512,512]{1,0:T(8,128)(2,1)}, bf16[512,512]{1,0:T(8,128)(2,1)S(1)}, u32[]{:S(2)}, u32[]{:S(2)}) collective-permute-start(bf16[512,512]{1,0:T(8,128)(2,1)} %dy_ref.7), channel_id=1, source_target_pairs={{0,12},{4,0},{8,4},{12,8},{1,13},{5,1},{9,5},{13,9},{2,14},{6,2},{... | collective-permute-start | bytes 1572872 | tf_op jit(solution)/shard_map/ppermute | solution.py:22
  28.0 1.6 %collective-permute-start.11 = (bf16[512,512]{1,0:T(8,128)(2,1)S(1)}, bf16[512,512]{1,0:T(8,128)(2,1)S(1)}, u32[]{:S(2)}, u32[]{:S(2)}) collective-permute-start(bf16[512,512]{1,0:T(8,128)(2,1)S(1)} %shard_map.172.own_ref.refs_4_), channel_id=1, source_target_pairs={{0,64},{64,128},{128,192},{192,0},{1,65},{65,129},{129,193},{193,1... | collective-permute-start | bytes 1572872 | tf_op jit(solution)/shard_map/ppermute | solution.py:22
  29.6 10.9 %collective-permute-done.7.left.refs_10_ = bf16[512,512]{1,0:T(8,128)(2,1)S(1)} collective-permute-done((bf16[512,512]{1,0:T(8,128)(2,1)}, bf16[512,512]{1,0:T(8,128)(2,1)S(1)}, u32[]{:S(2)}, u32[]{:S(2)}) %collective-permute-start.7) | collective-permute-done | bytes 524320 | tf_op jit(solution)/shard_map/ppermute | solution.py:22
  40.4 1.5 %collective-permute-done.6.z.refs_13_ = bf16[512,512]{1,0:T(8,128)(2,1)S(1)} collective-permute-done((bf16[512,512]{1,0:T(8,128)(2,1)}, bf16[512,512]{1,0:T(8,128)(2,1)S(1)}, u32[]{:S(2)}, u32[]{:S(2)}) %collective-permute-start.6) | collective-permute-done | bytes 524320 | tf_op jit(solution)/shard_map/ppermute | solution.py:22
  43.5 3.0 %collective-permute-start.10 = (bf16[768,512]{1,0:T(8,128)(2,1)}, bf16[768,512]{1,0:T(8,128)(2,1)}, u32[]{:S(2)}, u32[]{:S(2)}) collective-permute-start(bf16[768,512]{1,0:T(8,128)(2,1)} %get-tuple-element.51), channel_id=1, source_target_pairs={{0,12},{4,0},{8,4},{12,8},{1,13},{5,1},{9,5},{13,9},{2,14},{6,2},{... | collective-permute-start | bytes 2359304 | tf_op jit(solution)/shard_map/ppermute | solution.py:22
  46.5 3.0 %collective-permute-start.12 = (bf16[512,512]{1,0:T(8,128)(2,1)S(1)}, bf16[512,512]{1,0:T(8,128)(2,1)S(1)}, u32[]{:S(2)}, u32[]{:S(2)}) collective-permute-start(bf16[512,512]{1,0:T(8,128)(2,1)S(1)} %shard_map.172.own_ref.refs_4_), channel_id=1, source_target_pairs={{0,192},{64,0},{128,64},{192,128},{1,193},{65,1},{129,65},{193,129... | collective-permute-start | bytes 1572872 | tf_op jit(solution)/shard_map/ppermute | solution.py:22
  50.6 2.5 %shard_map.173 = bf16[512,512]{1,0:T(8,128)(2,1)S(1)} custom-call(s32[8]{0:T(128)S(1)} %stack.44.place_ref, bf16[512,8192]{1,0:T(8,128)(2,1)} %w_ref.7, bf16[512,8192]{1,0:T(8,128)(2,1)} %collective-permute-done.4.v_ref, bf16[512,512]{1,0:T(8,128)(2,1)S(1)} %copy-done.2, bf16[512,512]{1,0:T(8,128)(2,1)S(1)} %collective-permute-done.refs_1_), custom_call_target="tpu_custom_call" | custom-call | flops 536870912 | bytes 2621440 | tf_op jit(solution)/shard_map/pallas_call | solution.py:189
  53.6 5.6 %collective-permute-done.12.right_ref.refs_6_ = bf16[512,512]{1,0:T(8,128)(2,1)S(1)} collective-permute-done((bf16[512,512]{1,0:T(8,128)(2,1)S(1)}, bf16[512,512]{1,0:T(8,128)(2,1)S(1)}, u32[]{:S(2)}, u32[]{:S(2)}) %collective-permute-start.12) | collective-permute-done | bytes 524320 | tf_op jit(solution)/shard_map/ppermute | solution.py:22
  59.3 3.9 %collective-permute-start.14 = (bf16[256,512]{1,0:T(8,128)(2,1)S(1)}, bf16[256,512]{1,0:T(8,128)(2,1)S(1)}, u32[]{:S(2)}, u32[]{:S(2)}) collective-permute-start(bf16[256,512]{1,0:T(8,128)(2,1)S(1)} %slice.9), channel_id=1, source_target_pairs={{0,192},{64,0},{128,64},{192,128},{1,193},{65,1},{129,65},{193,129... | collective-permute-start | bytes 786440 | tf_op jit(solution)/shard_map/ppermute | solution.py:22
  63.2 1.9 %collective-permute-done.5.refs_2_ = bf16[512,512]{1,0:T(8,128)(2,1)S(1)} collective-permute-done((bf16[512,512]{1,0:T(8,128)(2,1)S(1)}, bf16[512,512]{1,0:T(8,128)(2,1)S(1)}, u32[]{:S(2)}, u32[]{:S(2)}) %collective-permute-start.5) | collective-permute-done | bytes 524320 | tf_op jit(solution)/shard_map/ppermute | solution.py:22
  65.2 4.1 %shard_map.174 = (bf16[768,512]{1,0:T(8,128)(2,1)S(1)}, bf16[768,512]{1,0:T(8,128)(2,1)S(1)}) custom-call(s32[8]{0:T(128)S(1)} %stack.44.place_ref, bf16[512,8192]{1,0:T(8,128)(2,1)} %w_ref.7, bf16[512,8192]{1,0:T(8,128)(2,1)} %collective-permute-done.4.v_ref, bf16[512,512]{1,0:T(8,128)(2,1)S(1)} %copy-done.2, ...), custom_call_target="tpu_custom_call" | custom-call | flops 1610612736 | bytes 6291456 | tf_op jit(solution)/shard_map/pallas_call | solution.py:189
  72.7 3.6 %collective-permute-done.16 = f32[32,512]{1,0:T(8,128)S(1)} collective-permute-done((f32[32,512]{1,0:T(8,128)S(1)}, f32[32,512]{1,0:T(8,128)S(1)}, u32[]{:S(2)}, u32[]{:S(2)}) %collective-permute-start.16) | collective-permute-done | bytes 65568 | tf_op jit(solution)/shard_map/ppermute | solution.py:22
  76.5 5.5 %collective-permute-done.17 = f32[32,512]{1,0:T(8,128)S(1)} collective-permute-done((f32[32,512]{1,0:T(8,128)S(1)}, f32[32,512]{1,0:T(8,128)S(1)}, u32[]{:S(2)}, u32[]{:S(2)}) %collective-permute-start.17) | collective-permute-done | bytes 65568 | tf_op jit(solution)/shard_map/ppermute | solution.py:22
  82.1 1.4 shard_map.176.refs_12_
  83.5 5.0 %collective-permute-done.18 = f32[32,512]{1,0:T(8,128)S(1)} collective-permute-done((f32[32,512]{1,0:T(8,128)S(1)}, f32[32,512]{1,0:T(8,128)S(1)}, u32[]{:S(2)}, u32[]{:S(2)}) %collective-permute-start.18) | collective-permute-done | bytes 65568 | tf_op jit(solution)/shard_map/ppermute | solution.py:22
  88.5 3.2 %collective-permute-start.21 = (bf16[768,512]{1,0:T(8,128)(2,1)S(1)}, bf16[768,512]{1,0:T(8,128)(2,1)S(1)}, u32[]{:S(2)}, u32[]{:S(2)}) collective-permute-start(bf16[768,512]{1,0:T(8,128)(2,1)S(1)} %get-tuple-element.56), channel_id=1, source_target_pairs={{0,12},{4,0},{8,4},{12,8},{1,13},{5,1},{9,5},{13,9},{2,14},{6,2},{... | collective-permute-start | bytes 2359304 | tf_op jit(solution)/shard_map/ppermute | solution.py:22
  92.9 3.2 %collective-permute-start.26 = (bf16[256,512]{1,0:T(8,128)(2,1)S(1)}, bf16[256,512]{1,0:T(8,128)(2,1)S(1)}, u32[]{:S(2)}, u32[]{:S(2)}) collective-permute-start(bf16[256,512]{1,0:T(8,128)(2,1)S(1)} %get-tuple-element.64), channel_id=1, source_target_pairs={{0,192},{64,0},{128,64},{192,128},{1,193},{65,1},{129,65},{193,129... | collective-permute-start | bytes 786440 | tf_op jit(solution)/shard_map/ppermute | solution.py:22
  96.2 4.3 %collective-permute-done.25.got_down_ref = bf16[256,512]{1,0:T(8,128)(2,1)S(1)} collective-permute-done((bf16[256,512]{1,0:T(8,128)(2,1)S(1)}, bf16[256,512]{1,0:T(8,128)(2,1)S(1)}, u32[]{:S(2)}, u32[]{:S(2)}) %collective-permute-start.25) | collective-permute-done | bytes 262176 | tf_op jit(solution)/shard_map/ppermute | solution.py:22
  102.0 3.8 %collective-permute-start.27 = (bf16[512,512]{1,0:T(8,128)(2,1)S(1)}, bf16[512,512]{1,0:T(8,128)(2,1)S(1)}, u32[]{:S(2)}, u32[]{:S(2)}) collective-permute-start(bf16[512,512]{1,0:T(8,128)(2,1)S(1)} %get-tuple-element.65), channel_id=1, source_target_pairs={{0,192},{64,0},{128,64},{192,128},{1,193},{65,1},{129,65},{193,129... | collective-permute-start | bytes 1572872 | tf_op jit(solution)/shard_map/ppermute | solution.py:22
  105.8 4.2 %shard_map.178 = (bf16[512,512]{1,0:T(8,128)(2,1)S(1)}, bf16[512,512]{1,0:T(8,128)(2,1)S(1)}, bf16[512,512]{1,0:T(8,128)(2,1)S(1)}) custom-call(s32[8]{0:T(128)S(1)} %stack.44.place_ref, bf16[512,8192]{1,0:T(8,128)(2,1)} %w_ref.7, bf16[512,8192]{1,0:T(8,128)(2,1)} %collective-permute-done.4.v_ref, bf16[512,512]{1,0:T(8,128)(2,1)S(1)} %copy-done.2, ...), custom_call_target="tpu_custom_call" | custom-call | flops 1610612736 | bytes 7340032 | tf_op jit(solution)/shard_map/pallas_call | solution.py:189
  110.0 2.5 %collective-permute-start.22 = (bf16[512,512]{1,0:T(8,128)(2,1)S(1)}, bf16[512,512]{1,0:T(8,128)(2,1)S(1)}, u32[]{:S(2)}, u32[]{:S(2)}) collective-permute-start(bf16[512,512]{1,0:T(8,128)(2,1)S(1)} %get-tuple-element.57), channel_id=1, source_target_pairs={{0,12},{4,0},{8,4},{12,8},{1,13},{5,1},{9,5},{13,9},{2,14},{6,2},{... | collective-permute-start | bytes 1572872 | tf_op jit(solution)/shard_map/ppermute | solution.py:22
  113.5 11.4 %shard_map.179 = (f32[512,512]{1,0:T(8,128)}, f32[512,512]{1,0:T(8,128)}, bf16[512,512]{1,0:T(8,128)(2,1)S(1)}) custom-call(s32[8]{0:T(128)S(1)} %stack.44.place_ref, bf16[512,8192]{1,0:T(8,128)(2,1)} %w_ref.7, bf16[512,8192]{1,0:T(8,128)(2,1)} %collective-permute-done.4.v_ref, bf16[512,512]{1,0:T(8,128)(2,1)S(1)} %copy-done.2, ...), custom_call_target="tpu_custom_call" | custom-call | flops 4294967296 | bytes 19988480 | tf_op jit(solution)/shard_map/pallas_call | solution.py:189
  126.8 3.0 %collective-permute-start.31 = (bf16[128,512]{1,0:T(8,128)(2,1)S(1)}, bf16[128,512]{1,0:T(8,128)(2,1)S(1)}, u32[]{:S(2)}, u32[]{:S(2)}) collective-permute-start(bf16[128,512]{1,0:T(8,128)(2,1)S(1)} %get-tuple-element.73), channel_id=1, source_target_pairs={{0,48},{16,0},{32,16},{48,32},{1,49},{17,1},{33,17},{49,33},{2,50}... | collective-permute-start | bytes 393224 | tf_op jit(solution)/shard_map/ppermute | solution.py:22
  129.9 2.2 %collective-permute-start.32 = (bf16[128,512]{1,0:T(8,128)(2,1)S(1)}, bf16[128,512]{1,0:T(8,128)(2,1)S(1)}, u32[]{:S(2)}, u32[]{:S(2)}) collective-permute-start(bf16[128,512]{1,0:T(8,128)(2,1)S(1)} %get-tuple-element.68), channel_id=1, source_target_pairs={{0,32},{16,48},{32,0},{48,16},{1,33},{17,49},{33,1},{49,17},{2,34}... | collective-permute-start | bytes 393224 | tf_op jit(solution)/shard_map/ppermute | solution.py:22
  136.4 2.4 %collective-permute-done.31.refs_2_ = bf16[128,512]{1,0:T(8,128)(2,1)S(1)} collective-permute-done((bf16[128,512]{1,0:T(8,128)(2,1)S(1)}, bf16[128,512]{1,0:T(8,128)(2,1)S(1)}, u32[]{:S(2)}, u32[]{:S(2)}) %collective-permute-start.31) | collective-permute-done | bytes 131104 | tf_op jit(solution)/shard_map/ppermute | solution.py:22
  138.8 4.8 %collective-permute-done.32.refs_3_ = bf16[128,512]{1,0:T(8,128)(2,1)S(1)} collective-permute-done((bf16[128,512]{1,0:T(8,128)(2,1)S(1)}, bf16[128,512]{1,0:T(8,128)(2,1)S(1)}, u32[]{:S(2)}, u32[]{:S(2)}) %collective-permute-start.32) | collective-permute-done | bytes 131104 | tf_op jit(solution)/shard_map/ppermute | solution.py:22
  (102 shorter events, 21.5 us)
Async XLA Ops:
  0.6 2.2 %collective-permute-start = (bf16[512,512]{1,0:T(8,128)(2,1)}, bf16[512,512]{1,0:T(8,128)(2,1)S(1)}, u32[]{:S(2)}, u32[]{:S(2)}) collective-permute-start(bf16[512,512]{1,0:T(8,128)(2,1)} %x_ref.7), channel_id=1, source_target_pairs={{0,1},{1,0},{2,3},{3,2},{4,5},{5,4},{6,7},{7,6},{8,9},{9,8},{10,11... | collective-permute-start | bytes 1572872 | tf_op jit(solution)/shard_map/ppermute | solution.py:22
  2.8 13.5 %collective-permute-start.1 = (bf16[128,512]{1,0:T(8,128)(2,1)S(1)}, bf16[128,512]{1,0:T(8,128)(2,1)S(1)}, u32[]{:S(2)}, u32[]{:S(2)}) collective-permute-start(bf16[128,512]{1,0:T(8,128)(2,1)S(1)} %shard_map.170.own), channel_id=1, source_target_pairs={{0,16},{16,32},{32,48},{48,0},{1,17},{17,33},{33,49},{49,1},{2,18}... | collective-permute-start | bytes 393224 | tf_op jit(solution)/shard_map/ppermute | solution.py:22
  6.1 10.2 %collective-permute-start.2 = (bf16[128,512]{1,0:T(8,128)(2,1)S(1)}, bf16[128,512]{1,0:T(8,128)(2,1)S(1)}, u32[]{:S(2)}, u32[]{:S(2)}) collective-permute-start(bf16[128,512]{1,0:T(8,128)(2,1)S(1)} %shard_map.170.own), channel_id=1, source_target_pairs={{0,48},{16,0},{32,16},{48,32},{1,49},{17,1},{33,17},{49,33},{2,50}... | collective-permute-start | bytes 393224 | tf_op jit(solution)/shard_map/ppermute | solution.py:22
  8.3 16.3 %collective-permute-start.3 = (bf16[128,512]{1,0:T(8,128)(2,1)S(1)}, bf16[128,512]{1,0:T(8,128)(2,1)S(1)}, u32[]{:S(2)}, u32[]{:S(2)}) collective-permute-start(bf16[128,512]{1,0:T(8,128)(2,1)S(1)} %shard_map.170.own), channel_id=1, source_target_pairs={{0,32},{16,48},{32,0},{48,16},{1,33},{17,49},{33,1},{49,17},{2,34}... | collective-permute-start | bytes 393224 | tf_op jit(solution)/shard_map/ppermute | solution.py:22
  24.6 25.0 %collective-permute-start.4 = (bf16[512,8192]{1,0:T(8,128)(2,1)}, bf16[512,8192]{1,0:T(8,128)(2,1)}, u32[]{:S(2)}, u32[]{:S(2)}) collective-permute-start(bf16[512,8192]{1,0:T(8,128)(2,1)} %w_ref.7), channel_id=1, source_target_pairs={{0,1},{1,0},{2,3},{3,2},{4,5},{5,4},{6,7},{7,6},{8,9},{9,8},{10,11... | collective-permute-start | bytes 25165832 | tf_op jit(solution)/shard_map/ppermute | solution.py:22
  24.7 15.8 %collective-permute-start.7 = (bf16[512,512]{1,0:T(8,128)(2,1)}, bf16[512,512]{1,0:T(8,128)(2,1)S(1)}, u32[]{:S(2)}, u32[]{:S(2)}) collective-permute-start(bf16[512,512]{1,0:T(8,128)(2,1)} %dy_ref.7), channel_id=1, source_target_pairs={{0,4},{4,8},{8,12},{12,0},{1,5},{5,9},{9,13},{13,1},{2,6},{6,10},{... | collective-permute-start | bytes 1572872 | tf_op jit(solution)/shard_map/ppermute | solution.py:22
  26.3 14.2 %collective-permute-start.8 = (bf16[512,512]{1,0:T(8,128)(2,1)}, bf16[512,512]{1,0:T(8,128)(2,1)S(1)}, u32[]{:S(2)}, u32[]{:S(2)}) collective-permute-start(bf16[512,512]{1,0:T(8,128)(2,1)} %dy_ref.7), channel_id=1, source_target_pairs={{0,12},{4,0},{8,4},{12,8},{1,13},{5,1},{9,5},{13,9},{2,14},{6,2},{... | collective-permute-start | bytes 1572872 | tf_op jit(solution)/shard_map/ppermute | solution.py:22
  28.0 13.9 %collective-permute-start.6 = (bf16[512,512]{1,0:T(8,128)(2,1)}, bf16[512,512]{1,0:T(8,128)(2,1)S(1)}, u32[]{:S(2)}, u32[]{:S(2)}) collective-permute-start(bf16[512,512]{1,0:T(8,128)(2,1)} %dy_ref.7), channel_id=1, source_target_pairs={{0,2},{2,0},{1,3},{3,1},{4,6},{6,4},{5,7},{7,5},{8,10},{10,8},{9,1... | collective-permute-start | bytes 1572872 | tf_op jit(solution)/shard_map/ppermute | solution.py:22
  28.0 25.5 %collective-permute-start.11 = (bf16[512,512]{1,0:T(8,128)(2,1)S(1)}, bf16[512,512]{1,0:T(8,128)(2,1)S(1)}, u32[]{:S(2)}, u32[]{:S(2)}) collective-permute-start(bf16[512,512]{1,0:T(8,128)(2,1)S(1)} %shard_map.172.own_ref.refs_4_), channel_id=1, source_target_pairs={{0,64},{64,128},{128,192},{192,0},{1,65},{65,129},{129,193},{193,1... | collective-permute-start | bytes 1572872 | tf_op jit(solution)/shard_map/ppermute | solution.py:22
  43.2 26.1 %collective-permute-start.9 = (bf16[768,512]{1,0:T(8,128)(2,1)}, bf16[768,512]{1,0:T(8,128)(2,1)}, u32[]{:S(2)}, u32[]{:S(2)}) collective-permute-start(bf16[768,512]{1,0:T(8,128)(2,1)} %get-tuple-element.50), channel_id=1, source_target_pairs={{0,4},{4,8},{8,12},{12,0},{1,5},{5,9},{9,13},{13,1},{2,6},{6,10},{... | collective-permute-start | bytes 2359304 | tf_op jit(solution)/shard_map/ppermute | solution.py:22
  43.5 25.8 %collective-permute-start.10 = (bf16[768,512]{1,0:T(8,128)(2,1)}, bf16[768,512]{1,0:T(8,128)(2,1)}, u32[]{:S(2)}, u32[]{:S(2)}) collective-permute-start(bf16[768,512]{1,0:T(8,128)(2,1)} %get-tuple-element.51), channel_id=1, source_target_pairs={{0,12},{4,0},{8,4},{12,8},{1,13},{5,1},{9,5},{13,9},{2,14},{6,2},{... | collective-permute-start | bytes 2359304 | tf_op jit(solution)/shard_map/ppermute | solution.py:22
  46.5 12.8 %collective-permute-start.12 = (bf16[512,512]{1,0:T(8,128)(2,1)S(1)}, bf16[512,512]{1,0:T(8,128)(2,1)S(1)}, u32[]{:S(2)}, u32[]{:S(2)}) collective-permute-start(bf16[512,512]{1,0:T(8,128)(2,1)S(1)} %shard_map.172.own_ref.refs_4_), channel_id=1, source_target_pairs={{0,192},{64,0},{128,64},{192,128},{1,193},{65,1},{129,65},{193,129... | collective-permute-start | bytes 1572872 | tf_op jit(solution)/shard_map/ppermute | solution.py:22
  53.1 12.1 %collective-permute-start.5 = (bf16[512,512]{1,0:T(8,128)(2,1)S(1)}, bf16[512,512]{1,0:T(8,128)(2,1)S(1)}, u32[]{:S(2)}, u32[]{:S(2)}) collective-permute-start(bf16[512,512]{1,0:T(8,128)(2,1)S(1)} %shard_map.173), channel_id=1, source_target_pairs={{0,2},{2,0},{1,3},{3,1},{4,6},{6,4},{5,7},{7,5},{8,10},{10,8},{9,1... | collective-permute-start | bytes 1572872 | tf_op jit(solution)/shard_map/ppermute | solution.py:22
  53.5 15.8 %collective-permute-start.13 = (bf16[256,512]{1,0:T(8,128)(2,1)S(1)}, bf16[256,512]{1,0:T(8,128)(2,1)S(1)}, u32[]{:S(2)}, u32[]{:S(2)}) collective-permute-start(bf16[256,512]{1,0:T(8,128)(2,1)S(1)} %slice.8), channel_id=1, source_target_pairs={{0,64},{64,128},{128,192},{192,0},{1,65},{65,129},{129,193},{193,1... | collective-permute-start | bytes 786440 | tf_op jit(solution)/shard_map/ppermute | solution.py:22
  59.3 10.0 %collective-permute-start.14 = (bf16[256,512]{1,0:T(8,128)(2,1)S(1)}, bf16[256,512]{1,0:T(8,128)(2,1)S(1)}, u32[]{:S(2)}, u32[]{:S(2)}) collective-permute-start(bf16[256,512]{1,0:T(8,128)(2,1)S(1)} %slice.9), channel_id=1, source_target_pairs={{0,192},{64,0},{128,64},{192,128},{1,193},{65,1},{129,65},{193,129... | collective-permute-start | bytes 786440 | tf_op jit(solution)/shard_map/ppermute | solution.py:22
  72.0 4.4 %collective-permute-start.16 = (f32[32,512]{1,0:T(8,128)S(1)}, f32[32,512]{1,0:T(8,128)S(1)}, u32[]{:S(2)}, u32[]{:S(2)}) collective-permute-start(f32[32,512]{1,0:T(8,128)S(1)} %add.133), channel_id=1, source_target_pairs={{0,2},{2,0},{1,3},{3,1},{4,6},{6,4},{5,7},{7,5},{8,10},{10,8},{9,1... | collective-permute-start | bytes 196616 | tf_op jit(solution)/shard_map/ppermute | solution.py:22
  76.4 5.6 %collective-permute-start.17 = (f32[32,512]{1,0:T(8,128)S(1)}, f32[32,512]{1,0:T(8,128)S(1)}, u32[]{:S(2)}, u32[]{:S(2)}) collective-permute-start(f32[32,512]{1,0:T(8,128)S(1)} %add.134), channel_id=1, source_target_pairs={{0,4},{4,8},{8,12},{12,0},{1,5},{5,9},{9,13},{13,1},{2,6},{6,10},{... | collective-permute-start | bytes 196616 | tf_op jit(solution)/shard_map/ppermute | solution.py:22
  82.0 6.5 %collective-permute-start.18 = (f32[32,512]{1,0:T(8,128)S(1)}, f32[32,512]{1,0:T(8,128)S(1)}, u32[]{:S(2)}, u32[]{:S(2)}) collective-permute-start(f32[32,512]{1,0:T(8,128)S(1)} %add.135), channel_id=1, source_target_pairs={{0,8},{4,12},{8,0},{12,4},{1,9},{5,13},{9,1},{13,5},{2,10},{6,14},... | collective-permute-start | bytes 196616 | tf_op jit(solution)/shard_map/ppermute | solution.py:22
  88.5 17.3 %collective-permute-start.19 = (bf16[768,512]{1,0:T(8,128)(2,1)S(1)}, bf16[768,512]{1,0:T(8,128)(2,1)S(1)}, u32[]{:S(2)}, u32[]{:S(2)}) collective-permute-start(bf16[768,512]{1,0:T(8,128)(2,1)S(1)} %get-tuple-element.53), channel_id=1, source_target_pairs={{0,4},{4,8},{8,12},{12,0},{1,5},{5,9},{9,13},{13,1},{2,6},{6,10},{... | collective-permute-start | bytes 2359304 | tf_op jit(solution)/shard_map/ppermute | solution.py:22
  88.5 17.3 %collective-permute-start.21 = (bf16[768,512]{1,0:T(8,128)(2,1)S(1)}, bf16[768,512]{1,0:T(8,128)(2,1)S(1)}, u32[]{:S(2)}, u32[]{:S(2)}) collective-permute-start(bf16[768,512]{1,0:T(8,128)(2,1)S(1)} %get-tuple-element.56), channel_id=1, source_target_pairs={{0,12},{4,0},{8,4},{12,8},{1,13},{5,1},{9,5},{13,9},{2,14},{6,2},{... | collective-permute-start | bytes 2359304 | tf_op jit(solution)/shard_map/ppermute | solution.py:22
  91.8 14.0 %collective-permute-start.20 = (bf16[512,512]{1,0:T(8,128)(2,1)S(1)}, bf16[512,512]{1,0:T(8,128)(2,1)S(1)}, u32[]{:S(2)}, u32[]{:S(2)}) collective-permute-start(bf16[512,512]{1,0:T(8,128)(2,1)S(1)} %shard_map.176.refs_12_), channel_id=1, source_target_pairs={{0,2},{2,0},{1,3},{3,1},{4,6},{6,4},{5,7},{7,5},{8,10},{10,8},{9,1... | collective-permute-start | bytes 1572872 | tf_op jit(solution)/shard_map/ppermute | solution.py:22
  92.8 7.7 %collective-permute-start.25 = (bf16[256,512]{1,0:T(8,128)(2,1)S(1)}, bf16[256,512]{1,0:T(8,128)(2,1)S(1)}, u32[]{:S(2)}, u32[]{:S(2)}) collective-permute-start(bf16[256,512]{1,0:T(8,128)(2,1)S(1)} %get-tuple-element.63), channel_id=1, source_target_pairs={{0,64},{64,128},{128,192},{192,0},{1,65},{65,129},{129,193},{193,1... | collective-permute-start | bytes 786440 | tf_op jit(solution)/shard_map/ppermute | solution.py:22
  92.9 8.3 %collective-permute-start.26 = (bf16[256,512]{1,0:T(8,128)(2,1)S(1)}, bf16[256,512]{1,0:T(8,128)(2,1)S(1)}, u32[]{:S(2)}, u32[]{:S(2)}) collective-permute-start(bf16[256,512]{1,0:T(8,128)(2,1)S(1)} %get-tuple-element.64), channel_id=1, source_target_pairs={{0,192},{64,0},{128,64},{192,128},{1,193},{65,1},{129,65},{193,129... | collective-permute-start | bytes 786440 | tf_op jit(solution)/shard_map/ppermute | solution.py:22
  102.0 23.0 %collective-permute-start.27 = (bf16[512,512]{1,0:T(8,128)(2,1)S(1)}, bf16[512,512]{1,0:T(8,128)(2,1)S(1)}, u32[]{:S(2)}, u32[]{:S(2)}) collective-permute-start(bf16[512,512]{1,0:T(8,128)(2,1)S(1)} %get-tuple-element.65), channel_id=1, source_target_pairs={{0,192},{64,0},{128,64},{192,128},{1,193},{65,1},{129,65},{193,129... | collective-permute-start | bytes 1572872 | tf_op jit(solution)/shard_map/ppermute | solution.py:22
  105.8 19.4 %collective-permute-start.28 = (bf16[512,512]{1,0:T(8,128)(2,1)S(1)}, bf16[512,512]{1,0:T(8,128)(2,1)S(1)}, u32[]{:S(2)}, u32[]{:S(2)}) collective-permute-start(bf16[512,512]{1,0:T(8,128)(2,1)S(1)} %get-tuple-element.67), channel_id=1, source_target_pairs={{0,64},{64,128},{128,192},{192,0},{1,65},{65,129},{129,193},{193,1... | collective-permute-start | bytes 1572872 | tf_op jit(solution)/shard_map/ppermute | solution.py:22
  110.0 15.1 %collective-permute-start.22 = (bf16[512,512]{1,0:T(8,128)(2,1)S(1)}, bf16[512,512]{1,0:T(8,128)(2,1)S(1)}, u32[]{:S(2)}, u32[]{:S(2)}) collective-permute-start(bf16[512,512]{1,0:T(8,128)(2,1)S(1)} %get-tuple-element.57), channel_id=1, source_target_pairs={{0,12},{4,0},{8,4},{12,8},{1,13},{5,1},{9,5},{13,9},{2,14},{6,2},{... | collective-permute-start | bytes 1572872 | tf_op jit(solution)/shard_map/ppermute | solution.py:22
  112.5 12.7 %collective-permute-start.23 = (bf16[512,512]{1,0:T(8,128)(2,1)S(1)}, bf16[512,512]{1,0:T(8,128)(2,1)S(1)}, u32[]{:S(2)}, u32[]{:S(2)}) collective-permute-start(bf16[512,512]{1,0:T(8,128)(2,1)S(1)} %get-tuple-element.58), channel_id=1, source_target_pairs={{0,4},{4,8},{8,12},{12,0},{1,5},{5,9},{9,13},{13,1},{2,6},{6,10},{... | collective-permute-start | bytes 1572872 | tf_op jit(solution)/shard_map/ppermute | solution.py:22
  112.5 12.7 %collective-permute-start.24 = (bf16[512,512]{1,0:T(8,128)(2,1)S(1)}, bf16[512,512]{1,0:T(8,128)(2,1)S(1)}, u32[]{:S(2)}, u32[]{:S(2)}) collective-permute-start(bf16[512,512]{1,0:T(8,128)(2,1)S(1)} %get-tuple-element.59), channel_id=1, source_target_pairs={{0,2},{2,0},{1,3},{3,1},{4,6},{6,4},{5,7},{7,5},{8,10},{10,8},{9,1... | collective-permute-start | bytes 1572872 | tf_op jit(solution)/shard_map/ppermute | solution.py:22
  125.0 9.3 %collective-permute-start.29 = (bf16[512,512]{1,0:T(8,128)(2,1)S(1)}, bf16[512,512]{1,0:T(8,128)(2,1)S(1)}, u32[]{:S(2)}, u32[]{:S(2)}) collective-permute-start(bf16[512,512]{1,0:T(8,128)(2,1)S(1)} %get-tuple-element.70), channel_id=1, source_target_pairs={{0,1},{1,0},{2,3},{3,2},{4,5},{5,4},{6,7},{7,6},{8,9},{9,8},{10,11... | collective-permute-start | bytes 1572872 | tf_op jit(solution)/shard_map/ppermute | solution.py:22
  125.6 10.7 %collective-permute-start.30 = (bf16[128,512]{1,0:T(8,128)(2,1)S(1)}, bf16[128,512]{1,0:T(8,128)(2,1)S(1)}, u32[]{:S(2)}, u32[]{:S(2)}) collective-permute-start(bf16[128,512]{1,0:T(8,128)(2,1)S(1)} %get-tuple-element.72), channel_id=1, source_target_pairs={{0,16},{16,32},{32,48},{48,0},{1,17},{17,33},{33,49},{49,1},{2,18}... | collective-permute-start | bytes 393224 | tf_op jit(solution)/shard_map/ppermute | solution.py:22
  126.8 12.0 %collective-permute-start.31 = (bf16[128,512]{1,0:T(8,128)(2,1)S(1)}, bf16[128,512]{1,0:T(8,128)(2,1)S(1)}, u32[]{:S(2)}, u32[]{:S(2)}) collective-permute-start(bf16[128,512]{1,0:T(8,128)(2,1)S(1)} %get-tuple-element.73), channel_id=1, source_target_pairs={{0,48},{16,0},{32,16},{48,32},{1,49},{17,1},{33,17},{49,33},{2,50}... | collective-permute-start | bytes 393224 | tf_op jit(solution)/shard_map/ppermute | solution.py:22
  129.9 13.7 %collective-permute-start.32 = (bf16[128,512]{1,0:T(8,128)(2,1)S(1)}, bf16[128,512]{1,0:T(8,128)(2,1)S(1)}, u32[]{:S(2)}, u32[]{:S(2)}) collective-permute-start(bf16[128,512]{1,0:T(8,128)(2,1)S(1)} %get-tuple-element.68), channel_id=1, source_target_pairs={{0,32},{16,48},{32,0},{48,16},{1,33},{17,49},{33,1},{49,17},{2,34}... | collective-permute-start | bytes 393224 | tf_op jit(solution)/shard_map/ppermute | solution.py:22
  (23 other events, 264.4 us)
where the time goes:
time: 146 us; the launch traced here: 145 us
  waiting for transfers between devices  56 us (38%)
  starting transfers between devices  48.2 us (33%)
  Pallas kernels  32.5 us (22%)
  local copies, waits for them, and re-layouts  6.79 us (5%)
    ppermute x33, waiting for transfers between devices, send(): return lax.ppermute(a, axis, [(i, (i + step) % n) for i in range(n)])  56 us
    ppermute x33, starting transfers between devices, send(): return lax.ppermute(a, axis, [(i, (i + step) % n) for i in range(n)])  48.2 us
    pallas_call x4, Pallas kernels, with_weight(): pl.pallas_call(run, in_specs=[pl.BlockSpec(memory_space=pltpu.SMEM)] + [p...  22.2 us
    pallas_call x11, Pallas kernels, call(): pl.pallas_call(body, out_shape=out, in_specs=[pl.BlockSpec(memory_space=p...  8.62 us
    unnamed x44, local copies, waits for them, and re-layouts  6.67 us
  transfers between devices with their start and end apart: 33, of which 14 were waited for; matrix products, arithmetic and copies ran while one was open for 0% of the time, Pallas kernels for 21%

commit v1 on v0

--- a/solution.py
+++ b/solution.py
@@ -145,7 +145,6 @@
     x, x2, m_ref, lb_ref, own_ref, left_ref, right_ref, far_d_ref, far_u_ref, *parts = ins
     lifted, own_out, other_out = outs
     n = far_d_ref.shape[0]
-    rows = x.shape[0]
     downs = [own_ref[:n], left_ref[:n], right_ref[:n], far_d_ref[...]]
     ups = [own_ref[n:], left_ref[n:], right_ref[n:], far_u_ref[...]]
     total = [None, None]
@@ -155,15 +154,9 @@
             total[which] = part if g == 0 else total[which] + part
     w, v = get(0, 0), get(0, 1)
     lifted[...] = 2.0 * total[0] + nn(x[...], w) + nn(x2[...], v)
-    first = parts[0][...]
-    own = 2.0 * total[1] + nt(first, w)
-    other = nt(first, v)
-    for i in range(1, 8):
-        part = parts[i][:rows]
-        own = own + nt(part, get(i, 0))
-        other = other + nt(part, get(i, 1))
-    own_out[...] = own
-    other_out[...] = other.astype(BF)
+    part, own, other = parts
+    own_out[...] = 2.0 * total[1] + own[...] + nt(part[...], get(1, 0))
+    other_out[...] = (other[...] + nt(part[...], get(1, 1))).astype(BF)
 
 
 def with_weight(body, blocks, w, other, places, ins, out, flops):
@@ -237,6 +230,27 @@
 def last_body(a, b, c, own, out):
     total = own[...] + a[...].astype(F32) + b[...].astype(F32) + c[...].astype(F32)
     out[...] = total.astype(BF)
+
+
+def back_near_body(get, ins, outs):
+    total = [None, None]
+    for i, part in enumerate(ins):
+        for j in range(2):
+            more = nt(part[...], get(i, j))
+            total[j] = more if total[j] is None else total[j] + more
+    for out, t in zip(outs, total):
+        out[...] = t
+
+
+def back_more_body(get, ins, outs):
+    *parts, own, other = ins
+    total = [own[...], other[...]]
+    for i, part in enumerate(parts):
+        rows = own.shape[0]
+        for j in range(2):
+            total[j] = total[j] + nt(part[:rows], get(i, j))
+    for out, t in zip(outs, total):
+        out[...] = t
 
 
 def pack_body(z, left, right, to_left, to_right):
@@ -324,29 +338,31 @@
     mask = token_mask(slots, counts, jnp.stack([iy, iz]).astype(jnp.int32), rank, per, toks)
     group = call(group_body, [shape(2 * n4, n, BF)], (tie(mine, mask), z_left, z_right, z_far))[0]
     y_left, y_right = send(group, "y", 1), send(group, "y", -1)
-    other = send(tie(w, group), "c", 1)
+    other = send(tie(w, group, d_left, d_right), "c", 1)
     d_z = send(tie(dy, group), "zl", 1)
-    to_left, to_right = call(pack_body, [pack] * 2, (d_z, d_left, d_right))
+    zf = weighed(first_body, (7,), (x, x2), [block])[0]
+    to_left, to_right = call(pack_body, [pack] * 2, (tie(d_z, y_left, y_right, zf), d_left, d_right))
+    a_left, a_right = send(to_right, "x", 1), send(to_left, "x", -1)
     y_far_d = send(y_left[:n4], "y", 1)
     y_far_u = send(y_right[n4:], "y", -1)
-    a_left, a_right = send(to_right, "x", 1), send(to_left, "x", -1)
-    zf = weighed(first_body, (7,), (x, x2), [block])[0]
     from_z = send(zf, "zl", 1)
-    p_left, p_right = weighed(far_body, (3, 5, 6), (x, x2, from_z), [pack] * 2)
+    p_left, p_right = weighed(far_body, (3, 5, 6), (x, x2, tie(from_z, y_far_d, y_far_u)), [pack] * 2)
     adapters = (group, y_left, y_right, y_far_d, y_far_u)
 
 
     lb = call(
         functools.partial(narrow_body, rank),
         [shape(2 * rank, toks, F32)],
-        (x, dy, tie(mask, p_left, a_left, a_right), *adapters),
+        (x, dy, tie(mask, p_left), *adapters),
         flops=4 * dot,
     )[0]
     lb = lb + send(lb, "c", 1)
-    lb = lb + send(lb, "zl", 1)
-    lb = lb + send(lb, "x", 1)
-    lb = lb + send(lb, "x", 2)
-    d_far = call(join_body, [block], (a_left, a_right))[0]
+    lb = tie(lb + send(lb, "zl", 1), a_left, a_right)
+    near = weighed(back_near_body, (0, 1, 2, 4), (tie(dy, lb), d_left, d_right, d_z), [wide] * 2)
+    lb = tie(lb, *near) + send(lb, "x", 1)
+    d_far = call(join_body, [block], (tie(a_left, lb), a_right))[0]
+    near = weighed(back_more_body, (3, 5, 6), (d_far, a_left, a_right, *near), [wide] * 2)
+    lb = tie(lb, *near) + send(lb, "x", 2)
 
     fd, fu = call(
         functools.partial(grad_far_body, rank),
@@ -366,24 +382,19 @@
     )
     got_l, got_r = send(g_left, "y", -1), send(g_right, "y", 1)
     left, right, z = weighed(near_body, (1, 2, 4), (x, x2, tie(b_left, d_zf), b_right), [block] * 3)
+    left, right, z = lax.optimization_barrier((left, right, z, got_l, got_r))[:3]
     sums = (send(left, "x", -1), send(right, "x", 1), send(z, "zl", 1))
     lifted, own_grad, to_other = weighed(
         functools.partial(back_body, rank),
-        tuple(range(8)),
+        (0, 7),
         (
             x,
             x2,
             mask,
             lb,
             *adapters,
-            tie(dy, left),
-            d_left,
-            d_right,
-            d_far,
-            d_z,
-            a_left,
-            a_right,
-            d_zf,
+            tie(d_zf, left),
+            *near,
         ),
         [wide, wide, block],
     )

time: 146 us -> 142 us (0.973)
  waiting for transfers between devices: 56 us -> 49.3 us
  Pallas kernels: 32.5 us -> 35.1 us
    ppermute x33, waiting for transfers between devices: 56 us -> 49.3 us  [send(): return lax.ppermute(a, axis, [(i, (i + step) % n) for i in range(n)])]
    pallas_call x4 -> x6, Pallas kernels: 22.2 us -> 26.3 us  [with_weight(): pl.pallas_call(run, in_specs=[pl.BlockSpec(memory_space=pltpu.SMEM)] + [p...]
    pallas_call x11, Pallas kernels: 8.62 us -> 7.08 us  [call(): pl.pallas_call(body, out_shape=out, in_specs=[pl.BlockSpec(memory_space=p...]
    unnamed x44 -> x42, local copies, waits for them, and re-layouts: 6.67 us -> 7.36 us
  transfers between devices with their start and end apart: 33 -> 33, of which waited for: 14 -> 17; matrix products, arithmetic and copies ran while one was open for 0% -> 0% of each run, Pallas kernels for 21% -> 24%
where the time goes in v1:
time: 142 us
  waiting for transfers between devices  49.3 us (35%)
  starting transfers between devices  48.6 us (34%)
  Pallas kernels  35.1 us (25%)
  local copies, waits for them, and re-layouts  7.48 us (5%)
    ppermute x33, waiting for transfers between devices, send(): return lax.ppermute(a, axis, [(i, (i + step) % n) for i in range(n)])  49.3 us
    ppermute x33, starting transfers between devices, send(): return lax.ppermute(a, axis, [(i, (i + step) % n) for i in range(n)])  48.6 us
    pallas_call x6, Pallas kernels, with_weight(): pl.pallas_call(run, in_specs=[pl.BlockSpec(memory_space=pltpu.SMEM)] + [p...  26.3 us
    unnamed x42, local copies, waits for them, and re-layouts  7.36 us
    pallas_call x11, Pallas kernels, call(): pl.pallas_call(body, out_shape=out, in_specs=[pl.BlockSpec(memory_space=p...  7.08 us
  transfers between devices with their start and end apart: 33, of which 17 were waited for; matrix products, arithmetic and copies ran while one was open for 0% of the time, Pallas kernels for 24%

profile of v1, /device:TPU:32, one launch (start us, length us, event | category | flops | bytes accessed | tf_op | source)
XLA Modules:
  0.0 141.6 jit_solution(6122463918291066065)
XLA Ops:
  2.3 1.7 %collective-permute-start.5 = (bf16[512,512]{1,0:T(8,128)(2,1)}, bf16[512,512]{1,0:T(8,128)(2,1)S(1)}, u32[]{:S(2)}, u32[]{:S(2)}) collective-permute-start(bf16[512,512]{1,0:T(8,128)(2,1)} %dy_ref.7), channel_id=1, source_target_pairs={{0,12},{4,0},{8,4},{12,8},{1,13},{5,1},{9,5},{13,9},{2,14},{6,2},{... | collective-permute-start | bytes 1572872 | tf_op jit(solution)/shard_map/ppermute | solution.py:22
  5.9 3.3 %collective-permute-start.1 = (bf16[128,512]{1,0:T(8,128)(2,1)S(1)}, bf16[128,512]{1,0:T(8,128)(2,1)S(1)}, u32[]{:S(2)}, u32[]{:S(2)}) collective-permute-start(bf16[128,512]{1,0:T(8,128)(2,1)S(1)} %shard_map.170.own), channel_id=1, source_target_pairs={{0,16},{16,32},{32,48},{48,0},{1,17},{17,33},{33,49},{49,1},{2,18}... | collective-permute-start | bytes 393224 | tf_op jit(solution)/shard_map/ppermute | solution.py:22
  9.2 2.2 %collective-permute-start.2 = (bf16[128,512]{1,0:T(8,128)(2,1)S(1)}, bf16[128,512]{1,0:T(8,128)(2,1)S(1)}, u32[]{:S(2)}, u32[]{:S(2)}) collective-permute-start(bf16[128,512]{1,0:T(8,128)(2,1)S(1)} %shard_map.170.own), channel_id=1, source_target_pairs={{0,48},{16,0},{32,16},{48,32},{1,49},{17,1},{33,17},{49,33},{2,50}... | collective-permute-start | bytes 393224 | tf_op jit(solution)/shard_map/ppermute | solution.py:22
  11.5 4.9 %collective-permute-start.3 = (bf16[128,512]{1,0:T(8,128)(2,1)S(1)}, bf16[128,512]{1,0:T(8,128)(2,1)S(1)}, u32[]{:S(2)}, u32[]{:S(2)}) collective-permute-start(bf16[128,512]{1,0:T(8,128)(2,1)S(1)} %shard_map.170.own), channel_id=1, source_target_pairs={{0,32},{16,48},{32,0},{48,16},{1,33},{17,49},{33,1},{49,17},{2,34}... | collective-permute-start | bytes 393224 | tf_op jit(solution)/shard_map/ppermute | solution.py:22
  17.8 1.7 %shard_map.171.m_ref.refs_2_ = bf16[1024,512]{1,0:T(8,128)(2,1)S(1)} custom-call(s32[1,64]{1,0:T(1,128)S(1)} %bitcast.43, s32[1,64]{1,0:T(1,128)S(1)} %copy-done.20, s32[2]{0:T(128)S(1)} %pad_add_fusion.place_ref), custom_call_target="tpu_custom_call" | custom-call | bytes 2097152 | tf_op jit(solution)/shard_map/pallas_call | solution.py:78
  19.5 7.8 %collective-permute-done.3.far = bf16[128,512]{1,0:T(8,128)(2,1)S(1)} collective-permute-done((bf16[128,512]{1,0:T(8,128)(2,1)S(1)}, bf16[128,512]{1,0:T(8,128)(2,1)S(1)}, u32[]{:S(2)}, u32[]{:S(2)}) %collective-permute-start.3) | collective-permute-done | bytes 131104 | tf_op jit(solution)/shard_map/ppermute | solution.py:22
  32.0 1.7 %collective-permute-start.10 = (bf16[512,512]{1,0:T(8,128)(2,1)S(1)}, bf16[512,512]{1,0:T(8,128)(2,1)S(1)}, u32[]{:S(2)}, u32[]{:S(2)}) collective-permute-start(bf16[512,512]{1,0:T(8,128)(2,1)S(1)} %shard_map.172.own_ref.refs_4_), channel_id=1, source_target_pairs={{0,192},{64,0},{128,64},{192,128},{1,193},{65,1},{129,65},{193,129... | collective-permute-start | bytes 1572872 | tf_op jit(solution)/shard_map/ppermute | solution.py:22
  33.8 10.2 %collective-permute-done.6.v_ref = bf16[512,8192]{1,0:T(8,128)(2,1)} collective-permute-done((bf16[512,8192]{1,0:T(8,128)(2,1)}, bf16[512,8192]{1,0:T(8,128)(2,1)}, u32[]{:S(2)}, u32[]{:S(2)}) %collective-permute-start.6) | collective-permute-done | bytes 8388640 | tf_op jit(solution)/shard_map/ppermute | solution.py:22
  45.0 2.5 %shard_map.173 = bf16[512,512]{1,0:T(8,128)(2,1)S(1)} custom-call(s32[8]{0:T(128)S(1)} %stack.44.place_ref, bf16[512,8192]{1,0:T(8,128)(2,1)} %w_ref.11, bf16[512,8192]{1,0:T(8,128)(2,1)} %collective-permute-done.6.v_ref, bf16[512,512]{1,0:T(8,128)(2,1)S(1)} %copy-done, bf16[512,512]{1,0:T(8,128)(2,1)S(1)} %collective-permute-done.refs_1_), custom_call_target="tpu_custom_call" | custom-call | flops 536870912 | bytes 2621440 | tf_op jit(solution)/shard_map/pallas_call | solution.py:182
  49.3 3.0 %collective-permute-start.16 = (bf16[768,512]{1,0:T(8,128)(2,1)S(1)}, bf16[768,512]{1,0:T(8,128)(2,1)S(1)}, u32[]{:S(2)}, u32[]{:S(2)}) collective-permute-start(bf16[768,512]{1,0:T(8,128)(2,1)S(1)} %get-tuple-element.68), channel_id=1, source_target_pairs={{0,12},{4,0},{8,4},{12,8},{1,13},{5,1},{9,5},{13,9},{2,14},{6,2},{... | collective-permute-start | bytes 2359304 | tf_op jit(solution)/shard_map/ppermute | solution.py:22
  53.8 2.1 %collective-permute-start.11 = (bf16[256,512]{1,0:T(8,128)(2,1)S(1)}, bf16[256,512]{1,0:T(8,128)(2,1)S(1)}, u32[]{:S(2)}, u32[]{:S(2)}) collective-permute-start(bf16[256,512]{1,0:T(8,128)(2,1)S(1)} %slice.9), channel_id=1, source_target_pairs={{0,192},{64,0},{128,64},{192,128},{1,193},{65,1},{129,65},{193,129... | collective-permute-start | bytes 786440 | tf_op jit(solution)/shard_map/ppermute | solution.py:22
  55.9 5.3 %collective-permute-done.9.far_d_ref.refs_7_ = bf16[256,512]{1,0:T(8,128)(2,1)S(1)} collective-permute-done((bf16[256,512]{1,0:T(8,128)(2,1)S(1)}, bf16[256,512]{1,0:T(8,128)(2,1)S(1)}, u32[]{:S(2)}, u32[]{:S(2)}) %collective-permute-start.9) | collective-permute-done | bytes 262176 | tf_op jit(solution)/shard_map/ppermute | solution.py:22
  61.6 4.1 %shard_map.174 = (bf16[768,512]{1,0:T(8,128)(2,1)S(1)}, bf16[768,512]{1,0:T(8,128)(2,1)S(1)}) custom-call(s32[8]{0:T(128)S(1)} %stack.44.place_ref, bf16[512,8192]{1,0:T(8,128)(2,1)} %w_ref.11, bf16[512,8192]{1,0:T(8,128)(2,1)} %collective-permute-done.6.v_ref, bf16[512,512]{1,0:T(8,128)(2,1)S(1)} %copy-done, ...), custom_call_target="tpu_custom_call" | custom-call | flops 1610612736 | bytes 6291456 | tf_op jit(solution)/shard_map/pallas_call | solution.py:182
  68.4 1.8 %collective-permute-start.15 = (f32[32,512]{1,0:T(8,128)S(1)}, f32[32,512]{1,0:T(8,128)S(1)}, u32[]{:S(2)}, u32[]{:S(2)}) collective-permute-start(f32[32,512]{1,0:T(8,128)S(1)} %add.133), channel_id=1, source_target_pairs={{0,2},{2,0},{1,3},{3,1},{4,6},{6,4},{5,7},{7,5},{8,10},{10,8},{9,1... | collective-permute-start | bytes 196616 | tf_op jit(solution)/shard_map/ppermute | solution.py:22
  70.2 2.6 %collective-permute-done.15 = f32[32,512]{1,0:T(8,128)S(1)} collective-permute-done((f32[32,512]{1,0:T(8,128)S(1)}, f32[32,512]{1,0:T(8,128)S(1)}, u32[]{:S(2)}, u32[]{:S(2)}) %collective-permute-start.15) | collective-permute-done | bytes 65568 | tf_op jit(solution)/shard_map/ppermute | solution.py:22
  73.1 5.6 %shard_map.177 = (f32[512,512]{1,0:T(8,128)S(1)}, f32[512,512]{1,0:T(8,128)S(1)}) custom-call(s32[8]{0:T(128)S(1)} %stack.44.place_ref, bf16[512,8192]{1,0:T(8,128)(2,1)} %w_ref.11, bf16[512,8192]{1,0:T(8,128)(2,1)} %collective-permute-done.6.v_ref, bf16[512,512]{1,0:T(8,128)(2,1)S(1)} %copy-done.2, bf16[512,512]{1,0:T(8,128)(2,1)S(1)} %copy-done.4, ...), custom_call_target="tpu_custom_call" | custom-call | flops 2147483648 | bytes 8388608 | tf_op jit(solution)/shard_map/pallas_call | solution.py:182
  78.7 2.8 %collective-permute-start.18 = (f32[32,512]{1,0:T(8,128)S(1)}, f32[32,512]{1,0:T(8,128)S(1)}, u32[]{:S(2)}, u32[]{:S(2)}) collective-permute-start(f32[32,512]{1,0:T(8,128)S(1)} %add.135), channel_id=1, source_target_pairs={{0,8},{4,12},{8,0},{12,4},{1,9},{5,13},{9,1},{13,5},{2,10},{6,14},... | collective-permute-start | bytes 196616 | tf_op jit(solution)/shard_map/ppermute | solution.py:22
  81.6 4.3 %shard_map.179 = (f32[512,512]{1,0:T(8,128)S(1)}, f32[512,512]{1,0:T(8,128)S(1)}) custom-call(s32[8]{0:T(128)S(1)} %stack.44.place_ref, bf16[512,8192]{1,0:T(8,128)(2,1)} %w_ref.11, bf16[512,8192]{1,0:T(8,128)(2,1)} %collective-permute-done.6.v_ref, bf16[512,512]{1,0:T(8,128)(2,1)S(1)} %shard_map.178.refs_0_, ...), custom_call_target="tpu_custom_call" | custom-call | flops 1610612736 | bytes 9437184 | tf_op jit(solution)/shard_map/pallas_call | solution.py:182
  87.1 2.1 %collective-permute-start.21 = (bf16[768,512]{1,0:T(8,128)(2,1)S(1)}, bf16[768,512]{1,0:T(8,128)(2,1)S(1)}, u32[]{:S(2)}, u32[]{:S(2)}) collective-permute-start(bf16[768,512]{1,0:T(8,128)(2,1)S(1)} %get-tuple-element.81), channel_id=1, source_target_pairs={{0,12},{4,0},{8,4},{12,8},{1,13},{5,1},{9,5},{13,9},{2,14},{6,2},{... | collective-permute-start | bytes 2359304 | tf_op jit(solution)/shard_map/ppermute | solution.py:22
  89.7 1.6 %collective-permute-start.22 = (bf16[256,512]{1,0:T(8,128)(2,1)S(1)}, bf16[256,512]{1,0:T(8,128)(2,1)S(1)}, u32[]{:S(2)}, u32[]{:S(2)}) collective-permute-start(bf16[256,512]{1,0:T(8,128)(2,1)S(1)} %get-tuple-element.85), channel_id=1, source_target_pairs={{0,64},{64,128},{128,192},{192,0},{1,65},{65,129},{129,193},{193,1... | collective-permute-start | bytes 786440 | tf_op jit(solution)/shard_map/ppermute | solution.py:22
  91.3 1.7 %collective-permute-start.23 = (bf16[256,512]{1,0:T(8,128)(2,1)S(1)}, bf16[256,512]{1,0:T(8,128)(2,1)S(1)}, u32[]{:S(2)}, u32[]{:S(2)}) collective-permute-start(bf16[256,512]{1,0:T(8,128)(2,1)S(1)} %get-tuple-element.86), channel_id=1, source_target_pairs={{0,192},{64,0},{128,64},{192,128},{1,193},{65,1},{129,65},{193,129... | collective-permute-start | bytes 786440 | tf_op jit(solution)/shard_map/ppermute | solution.py:22
  93.5 3.8 %collective-permute-done.22.got_down_ref = bf16[256,512]{1,0:T(8,128)(2,1)S(1)} collective-permute-done((bf16[256,512]{1,0:T(8,128)(2,1)S(1)}, bf16[256,512]{1,0:T(8,128)(2,1)S(1)}, u32[]{:S(2)}, u32[]{:S(2)}) %collective-permute-start.22) | collective-permute-done | bytes 262176 | tf_op jit(solution)/shard_map/ppermute | solution.py:22
  98.4 3.0 %collective-permute-start.24 = (bf16[512,512]{1,0:T(8,128)(2,1)S(1)}, bf16[512,512]{1,0:T(8,128)(2,1)S(1)}, u32[]{:S(2)}, u32[]{:S(2)}) collective-permute-start(bf16[512,512]{1,0:T(8,128)(2,1)S(1)} %get-tuple-element.87), channel_id=1, source_target_pairs={{0,192},{64,0},{128,64},{192,128},{1,193},{65,1},{129,65},{193,129... | collective-permute-start | bytes 1572872 | tf_op jit(solution)/shard_map/ppermute | solution.py:22
  101.4 2.9 %collective-permute-done.20.refs_9_ = bf16[512,512]{1,0:T(8,128)(2,1)S(1)} collective-permute-done((bf16[512,512]{1,0:T(8,128)(2,1)S(1)}, bf16[512,512]{1,0:T(8,128)(2,1)S(1)}, u32[]{:S(2)}, u32[]{:S(2)}) %collective-permute-start.20) | collective-permute-done | bytes 524320 | tf_op jit(solution)/shard_map/ppermute | solution.py:22
  105.1 4.2 %shard_map.180 = (bf16[512,512]{1,0:T(8,128)(2,1)S(1)}, bf16[512,512]{1,0:T(8,128)(2,1)S(1)}, bf16[512,512]{1,0:T(8,128)(2,1)S(1)}) custom-call(s32[8]{0:T(128)S(1)} %stack.44.place_ref, bf16[512,8192]{1,0:T(8,128)(2,1)} %w_ref.11, bf16[512,8192]{1,0:T(8,128)(2,1)} %collective-permute-done.6.v_ref, bf16[512,512]{1,0:T(8,128)(2,1)S(1)} %copy-done.1, ...), custom_call_target="tpu_custom_call" | custom-call | flops 1610612736 | bytes 7340032 | tf_op jit(solution)/shard_map/pallas_call | solution.py:182
  109.6 3.4 %collective-permute-done.25.b_ref = bf16[512,512]{1,0:T(8,128)(2,1)S(1)} collective-permute-done((bf16[512,512]{1,0:T(8,128)(2,1)S(1)}, bf16[512,512]{1,0:T(8,128)(2,1)S(1)}, u32[]{:S(2)}, u32[]{:S(2)}) %collective-permute-start.25) | collective-permute-done | bytes 524320 | tf_op jit(solution)/shard_map/ppermute | solution.py:22
  113.3 1.7 %collective-permute-start.27 = (bf16[512,512]{1,0:T(8,128)(2,1)S(1)}, bf16[512,512]{1,0:T(8,128)(2,1)S(1)}, u32[]{:S(2)}, u32[]{:S(2)}) collective-permute-start(bf16[512,512]{1,0:T(8,128)(2,1)S(1)} %get-tuple-element.90), channel_id=1, source_target_pairs={{0,4},{4,8},{8,12},{12,0},{1,5},{5,9},{9,13},{13,1},{2,6},{6,10},{... | collective-permute-start | bytes 1572872 | tf_op jit(solution)/shard_map/ppermute | solution.py:22
  115.8 5.7 %shard_map.183 = (f32[512,512]{1,0:T(8,128)S(1)}, f32[512,512]{1,0:T(8,128)S(1)}, bf16[512,512]{1,0:T(8,128)(2,1)S(1)}) custom-call(s32[8]{0:T(128)S(1)} %stack.44.place_ref, bf16[512,8192]{1,0:T(8,128)(2,1)} %w_ref.11, bf16[512,8192]{1,0:T(8,128)(2,1)} %collective-permute-done.6.v_ref, bf16[512,512]{1,0:T(8,128)(2,1)S(1)} %copy-done.1, ...), custom_call_target="tpu_custom_call" | custom-call | flops 1073741824 | bytes 11599872 | tf_op jit(solution)/shard_map/pallas_call | solution.py:182
  122.5 1.8 %collective-permute-done.27.b = bf16[512,512]{1,0:T(8,128)(2,1)S(1)} collective-permute-done((bf16[512,512]{1,0:T(8,128)(2,1)S(1)}, bf16[512,512]{1,0:T(8,128)(2,1)S(1)}, u32[]{:S(2)}, u32[]{:S(2)}) %collective-permute-start.27) | collective-permute-done | bytes 524320 | tf_op jit(solution)/shard_map/ppermute | solution.py:22
  126.2 2.9 %collective-permute-start.31 = (bf16[128,512]{1,0:T(8,128)(2,1)S(1)}, bf16[128,512]{1,0:T(8,128)(2,1)S(1)}, u32[]{:S(2)}, u32[]{:S(2)}) collective-permute-start(bf16[128,512]{1,0:T(8,128)(2,1)S(1)} %get-tuple-element.101), channel_id=1, source_target_pairs={{0,48},{16,0},{32,16},{48,32},{1,49},{17,1},{33,17},{49,33},{2,50}... | collective-permute-start | bytes 393224 | tf_op jit(solution)/shard_map/ppermute | solution.py:22
  129.0 2.2 %collective-permute-start.32 = (bf16[128,512]{1,0:T(8,128)(2,1)S(1)}, bf16[128,512]{1,0:T(8,128)(2,1)S(1)}, u32[]{:S(2)}, u32[]{:S(2)}) collective-permute-start(bf16[128,512]{1,0:T(8,128)(2,1)S(1)} %get-tuple-element.96), channel_id=1, source_target_pairs={{0,32},{16,48},{32,0},{48,16},{1,33},{17,49},{33,1},{49,17},{2,34}... | collective-permute-start | bytes 393224 | tf_op jit(solution)/shard_map/ppermute | solution.py:22
  133.1 6.5 %collective-permute-done.30.refs_1_ = bf16[128,512]{1,0:T(8,128)(2,1)S(1)} collective-permute-done((bf16[128,512]{1,0:T(8,128)(2,1)S(1)}, bf16[128,512]{1,0:T(8,128)(2,1)S(1)}, u32[]{:S(2)}, u32[]{:S(2)}) %collective-permute-start.30) | collective-permute-done | bytes 131104 | tf_op jit(solution)/shard_map/ppermute | solution.py:22
  (102 shorter events, 29.5 us)
Async XLA Ops:
  0.6 5.2 %collective-permute-start = (bf16[512,512]{1,0:T(8,128)(2,1)}, bf16[512,512]{1,0:T(8,128)(2,1)S(1)}, u32[]{:S(2)}, u32[]{:S(2)}) collective-permute-start(bf16[512,512]{1,0:T(8,128)(2,1)} %x_ref.7), channel_id=1, source_target_pairs={{0,1},{1,0},{2,3},{3,2},{4,5},{5,4},{6,7},{7,6},{8,9},{9,8},{10,11... | collective-permute-start | bytes 1572872 | tf_op jit(solution)/shard_map/ppermute | solution.py:22
  0.7 28.1 %collective-permute-start.4 = (bf16[512,512]{1,0:T(8,128)(2,1)}, bf16[512,512]{1,0:T(8,128)(2,1)S(1)}, u32[]{:S(2)}, u32[]{:S(2)}) collective-permute-start(bf16[512,512]{1,0:T(8,128)(2,1)} %dy_ref.7), channel_id=1, source_target_pairs={{0,4},{4,8},{8,12},{12,0},{1,5},{5,9},{9,13},{13,1},{2,6},{6,10},{... | collective-permute-start | bytes 1572872 | tf_op jit(solution)/shard_map/ppermute | solution.py:22
  2.3 27.3 %collective-permute-start.5 = (bf16[512,512]{1,0:T(8,128)(2,1)}, bf16[512,512]{1,0:T(8,128)(2,1)S(1)}, u32[]{:S(2)}, u32[]{:S(2)}) collective-permute-start(bf16[512,512]{1,0:T(8,128)(2,1)} %dy_ref.7), channel_id=1, source_target_pairs={{0,12},{4,0},{8,4},{12,8},{1,13},{5,1},{9,5},{13,9},{2,14},{6,2},{... | collective-permute-start | bytes 1572872 | tf_op jit(solution)/shard_map/ppermute | solution.py:22
  5.9 13.6 %collective-permute-start.1 = (bf16[128,512]{1,0:T(8,128)(2,1)S(1)}, bf16[128,512]{1,0:T(8,128)(2,1)S(1)}, u32[]{:S(2)}, u32[]{:S(2)}) collective-permute-start(bf16[128,512]{1,0:T(8,128)(2,1)S(1)} %shard_map.170.own), channel_id=1, source_target_pairs={{0,16},{16,32},{32,48},{48,0},{1,17},{17,33},{33,49},{49,1},{2,18}... | collective-permute-start | bytes 393224 | tf_op jit(solution)/shard_map/ppermute | solution.py:22
  9.2 10.2 %collective-permute-start.2 = (bf16[128,512]{1,0:T(8,128)(2,1)S(1)}, bf16[128,512]{1,0:T(8,128)(2,1)S(1)}, u32[]{:S(2)}, u32[]{:S(2)}) collective-permute-start(bf16[128,512]{1,0:T(8,128)(2,1)S(1)} %shard_map.170.own), channel_id=1, source_target_pairs={{0,48},{16,0},{32,16},{48,32},{1,49},{17,1},{33,17},{49,33},{2,50}... | collective-permute-start | bytes 393224 | tf_op jit(solution)/shard_map/ppermute | solution.py:22
  11.5 15.8 %collective-permute-start.3 = (bf16[128,512]{1,0:T(8,128)(2,1)S(1)}, bf16[128,512]{1,0:T(8,128)(2,1)S(1)}, u32[]{:S(2)}, u32[]{:S(2)}) collective-permute-start(bf16[128,512]{1,0:T(8,128)(2,1)S(1)} %shard_map.170.own), channel_id=1, source_target_pairs={{0,32},{16,48},{32,0},{48,16},{1,33},{17,49},{33,1},{49,17},{2,34}... | collective-permute-start | bytes 393224 | tf_op jit(solution)/shard_map/ppermute | solution.py:22
  30.4 13.5 %collective-permute-start.6 = (bf16[512,8192]{1,0:T(8,128)(2,1)}, bf16[512,8192]{1,0:T(8,128)(2,1)}, u32[]{:S(2)}, u32[]{:S(2)}) collective-permute-start(bf16[512,8192]{1,0:T(8,128)(2,1)} %w_ref.11), channel_id=1, source_target_pairs={{0,1},{1,0},{2,3},{3,2},{4,5},{5,4},{6,7},{7,6},{8,9},{9,8},{10,11... | collective-permute-start | bytes 25165832 | tf_op jit(solution)/shard_map/ppermute | solution.py:22
  30.4 17.1 %collective-permute-start.8 = (bf16[512,512]{1,0:T(8,128)(2,1)S(1)}, bf16[512,512]{1,0:T(8,128)(2,1)S(1)}, u32[]{:S(2)}, u32[]{:S(2)}) collective-permute-start(bf16[512,512]{1,0:T(8,128)(2,1)S(1)} %shard_map.172.own_ref.refs_4_), channel_id=1, source_target_pairs={{0,64},{64,128},{128,192},{192,0},{1,65},{65,129},{129,193},{193,1... | collective-permute-start | bytes 1572872 | tf_op jit(solution)/shard_map/ppermute | solution.py:22
  32.0 15.6 %collective-permute-start.10 = (bf16[512,512]{1,0:T(8,128)(2,1)S(1)}, bf16[512,512]{1,0:T(8,128)(2,1)S(1)}, u32[]{:S(2)}, u32[]{:S(2)}) collective-permute-start(bf16[512,512]{1,0:T(8,128)(2,1)S(1)} %shard_map.172.own_ref.refs_4_), channel_id=1, source_target_pairs={{0,192},{64,0},{128,64},{192,128},{1,193},{65,1},{129,65},{193,129... | collective-permute-start | bytes 1572872 | tf_op jit(solution)/shard_map/ppermute | solution.py:22
  33.7 14.2 %collective-permute-start.12 = (bf16[512,512]{1,0:T(8,128)(2,1)}, bf16[512,512]{1,0:T(8,128)(2,1)}, u32[]{:S(2)}, u32[]{:S(2)}) collective-permute-start(bf16[512,512]{1,0:T(8,128)(2,1)} %dy_ref.7), channel_id=1, source_target_pairs={{0,2},{2,0},{1,3},{3,1},{4,6},{6,4},{5,7},{7,5},{8,10},{10,8},{9,1... | collective-permute-start | bytes 1572872 | tf_op jit(solution)/shard_map/ppermute | solution.py:22
  47.5 14.1 %collective-permute-start.7 = (bf16[512,512]{1,0:T(8,128)(2,1)S(1)}, bf16[512,512]{1,0:T(8,128)(2,1)S(1)}, u32[]{:S(2)}, u32[]{:S(2)}) collective-permute-start(bf16[512,512]{1,0:T(8,128)(2,1)S(1)} %shard_map.173), channel_id=1, source_target_pairs={{0,2},{2,0},{1,3},{3,1},{4,6},{6,4},{5,7},{7,5},{8,10},{10,8},{9,1... | collective-permute-start | bytes 1572872 | tf_op jit(solution)/shard_map/ppermute | solution.py:22
  49.0 23.7 %collective-permute-start.13 = (bf16[768,512]{1,0:T(8,128)(2,1)S(1)}, bf16[768,512]{1,0:T(8,128)(2,1)S(1)}, u32[]{:S(2)}, u32[]{:S(2)}) collective-permute-start(bf16[768,512]{1,0:T(8,128)(2,1)S(1)} %get-tuple-element.66), channel_id=1, source_target_pairs={{0,4},{4,8},{8,12},{12,0},{1,5},{5,9},{9,13},{13,1},{2,6},{6,10},{... | collective-permute-start | bytes 2359304 | tf_op jit(solution)/shard_map/ppermute | solution.py:22
  49.3 23.4 %collective-permute-start.16 = (bf16[768,512]{1,0:T(8,128)(2,1)S(1)}, bf16[768,512]{1,0:T(8,128)(2,1)S(1)}, u32[]{:S(2)}, u32[]{:S(2)}) collective-permute-start(bf16[768,512]{1,0:T(8,128)(2,1)S(1)} %get-tuple-element.68), channel_id=1, source_target_pairs={{0,12},{4,0},{8,4},{12,8},{1,13},{5,1},{9,5},{13,9},{2,14},{6,2},{... | collective-permute-start | bytes 2359304 | tf_op jit(solution)/shard_map/ppermute | solution.py:22
  52.3 8.9 %collective-permute-start.9 = (bf16[256,512]{1,0:T(8,128)(2,1)S(1)}, bf16[256,512]{1,0:T(8,128)(2,1)S(1)}, u32[]{:S(2)}, u32[]{:S(2)}) collective-permute-start(bf16[256,512]{1,0:T(8,128)(2,1)S(1)} %slice.8), channel_id=1, source_target_pairs={{0,64},{64,128},{128,192},{192,0},{1,65},{65,129},{129,193},{193,1... | collective-permute-start | bytes 786440 | tf_op jit(solution)/shard_map/ppermute | solution.py:22
  53.8 7.8 %collective-permute-start.11 = (bf16[256,512]{1,0:T(8,128)(2,1)S(1)}, bf16[256,512]{1,0:T(8,128)(2,1)S(1)}, u32[]{:S(2)}, u32[]{:S(2)}) collective-permute-start(bf16[256,512]{1,0:T(8,128)(2,1)S(1)} %slice.9), channel_id=1, source_target_pairs={{0,192},{64,0},{128,64},{192,128},{1,193},{65,1},{129,65},{193,129... | collective-permute-start | bytes 786440 | tf_op jit(solution)/shard_map/ppermute | solution.py:22
  68.4 4.4 %collective-permute-start.15 = (f32[32,512]{1,0:T(8,128)S(1)}, f32[32,512]{1,0:T(8,128)S(1)}, u32[]{:S(2)}, u32[]{:S(2)}) collective-permute-start(f32[32,512]{1,0:T(8,128)S(1)} %add.133), channel_id=1, source_target_pairs={{0,2},{2,0},{1,3},{3,1},{4,6},{6,4},{5,7},{7,5},{8,10},{10,8},{9,1... | collective-permute-start | bytes 196616 | tf_op jit(solution)/shard_map/ppermute | solution.py:22
  72.7 5.9 %collective-permute-start.17 = (f32[32,512]{1,0:T(8,128)S(1)}, f32[32,512]{1,0:T(8,128)S(1)}, u32[]{:S(2)}, u32[]{:S(2)}) collective-permute-start(f32[32,512]{1,0:T(8,128)S(1)} %add.134), channel_id=1, source_target_pairs={{0,4},{4,8},{8,12},{12,0},{1,5},{5,9},{9,13},{13,1},{2,6},{6,10},{... | collective-permute-start | bytes 196616 | tf_op jit(solution)/shard_map/ppermute | solution.py:22
  78.7 7.2 %collective-permute-start.18 = (f32[32,512]{1,0:T(8,128)S(1)}, f32[32,512]{1,0:T(8,128)S(1)}, u32[]{:S(2)}, u32[]{:S(2)}) collective-permute-start(f32[32,512]{1,0:T(8,128)S(1)} %add.135), channel_id=1, source_target_pairs={{0,8},{4,12},{8,0},{12,4},{1,9},{5,13},{9,1},{13,5},{2,10},{6,14},... | collective-permute-start | bytes 196616 | tf_op jit(solution)/shard_map/ppermute | solution.py:22
  85.9 19.2 %collective-permute-start.19 = (bf16[768,512]{1,0:T(8,128)(2,1)S(1)}, bf16[768,512]{1,0:T(8,128)(2,1)S(1)}, u32[]{:S(2)}, u32[]{:S(2)}) collective-permute-start(bf16[768,512]{1,0:T(8,128)(2,1)S(1)} %get-tuple-element.78), channel_id=1, source_target_pairs={{0,4},{4,8},{8,12},{12,0},{1,5},{5,9},{9,13},{13,1},{2,6},{6,10},{... | collective-permute-start | bytes 2359304 | tf_op jit(solution)/shard_map/ppermute | solution.py:22
  87.1 18.0 %collective-permute-start.21 = (bf16[768,512]{1,0:T(8,128)(2,1)S(1)}, bf16[768,512]{1,0:T(8,128)(2,1)S(1)}, u32[]{:S(2)}, u32[]{:S(2)}) collective-permute-start(bf16[768,512]{1,0:T(8,128)(2,1)S(1)} %get-tuple-element.81), channel_id=1, source_target_pairs={{0,12},{4,0},{8,4},{12,8},{1,13},{5,1},{9,5},{13,9},{2,14},{6,2},{... | collective-permute-start | bytes 2359304 | tf_op jit(solution)/shard_map/ppermute | solution.py:22
  89.7 7.7 %collective-permute-start.22 = (bf16[256,512]{1,0:T(8,128)(2,1)S(1)}, bf16[256,512]{1,0:T(8,128)(2,1)S(1)}, u32[]{:S(2)}, u32[]{:S(2)}) collective-permute-start(bf16[256,512]{1,0:T(8,128)(2,1)S(1)} %get-tuple-element.85), channel_id=1, source_target_pairs={{0,64},{64,128},{128,192},{192,0},{1,65},{65,129},{129,193},{193,1... | collective-permute-start | bytes 786440 | tf_op jit(solution)/shard_map/ppermute | solution.py:22
  91.3 6.4 %collective-permute-start.23 = (bf16[256,512]{1,0:T(8,128)(2,1)S(1)}, bf16[256,512]{1,0:T(8,128)(2,1)S(1)}, u32[]{:S(2)}, u32[]{:S(2)}) collective-permute-start(bf16[256,512]{1,0:T(8,128)(2,1)S(1)} %get-tuple-element.86), channel_id=1, source_target_pairs={{0,192},{64,0},{128,64},{192,128},{1,193},{65,1},{129,65},{193,129... | collective-permute-start | bytes 786440 | tf_op jit(solution)/shard_map/ppermute | solution.py:22
  93.0 11.3 %collective-permute-start.20 = (bf16[512,512]{1,0:T(8,128)(2,1)S(1)}, bf16[512,512]{1,0:T(8,128)(2,1)S(1)}, u32[]{:S(2)}, u32[]{:S(2)}) collective-permute-start(bf16[512,512]{1,0:T(8,128)(2,1)S(1)} %shard_map.178.refs_0_), channel_id=1, source_target_pairs={{0,2},{2,0},{1,3},{3,1},{4,6},{6,4},{5,7},{7,5},{8,10},{10,8},{9,1... | collective-permute-start | bytes 1572872 | tf_op jit(solution)/shard_map/ppermute | solution.py:22
  98.4 11.2 %collective-permute-start.24 = (bf16[512,512]{1,0:T(8,128)(2,1)S(1)}, bf16[512,512]{1,0:T(8,128)(2,1)S(1)}, u32[]{:S(2)}, u32[]{:S(2)}) collective-permute-start(bf16[512,512]{1,0:T(8,128)(2,1)S(1)} %get-tuple-element.87), channel_id=1, source_target_pairs={{0,192},{64,0},{128,64},{192,128},{1,193},{65,1},{129,65},{193,129... | collective-permute-start | bytes 1572872 | tf_op jit(solution)/shard_map/ppermute | solution.py:22
  101.4 11.7 %collective-permute-start.25 = (bf16[512,512]{1,0:T(8,128)(2,1)S(1)}, bf16[512,512]{1,0:T(8,128)(2,1)S(1)}, u32[]{:S(2)}, u32[]{:S(2)}) collective-permute-start(bf16[512,512]{1,0:T(8,128)(2,1)S(1)} %get-tuple-element.88), channel_id=1, source_target_pairs={{0,64},{64,128},{128,192},{192,0},{1,65},{65,129},{129,193},{193,1... | collective-permute-start | bytes 1572872 | tf_op jit(solution)/shard_map/ppermute | solution.py:22
  113.0 9.5 %collective-permute-start.26 = (bf16[512,512]{1,0:T(8,128)(2,1)S(1)}, bf16[512,512]{1,0:T(8,128)(2,1)S(1)}, u32[]{:S(2)}, u32[]{:S(2)}) collective-permute-start(bf16[512,512]{1,0:T(8,128)(2,1)S(1)} %get-tuple-element.89), channel_id=1, source_target_pairs={{0,12},{4,0},{8,4},{12,8},{1,13},{5,1},{9,5},{13,9},{2,14},{6,2},{... | collective-permute-start | bytes 1572872 | tf_op jit(solution)/shard_map/ppermute | solution.py:22
  113.3 11.0 %collective-permute-start.27 = (bf16[512,512]{1,0:T(8,128)(2,1)S(1)}, bf16[512,512]{1,0:T(8,128)(2,1)S(1)}, u32[]{:S(2)}, u32[]{:S(2)}) collective-permute-start(bf16[512,512]{1,0:T(8,128)(2,1)S(1)} %get-tuple-element.90), channel_id=1, source_target_pairs={{0,4},{4,8},{8,12},{12,0},{1,5},{5,9},{9,13},{13,1},{2,6},{6,10},{... | collective-permute-start | bytes 1572872 | tf_op jit(solution)/shard_map/ppermute | solution.py:22
  115.0 9.3 %collective-permute-start.28 = (bf16[512,512]{1,0:T(8,128)(2,1)S(1)}, bf16[512,512]{1,0:T(8,128)(2,1)S(1)}, u32[]{:S(2)}, u32[]{:S(2)}) collective-permute-start(bf16[512,512]{1,0:T(8,128)(2,1)S(1)} %get-tuple-element.91), channel_id=1, source_target_pairs={{0,2},{2,0},{1,3},{3,1},{4,6},{6,4},{5,7},{7,5},{8,10},{10,8},{9,1... | collective-permute-start | bytes 1572872 | tf_op jit(solution)/shard_map/ppermute | solution.py:22
  121.6 10.6 %collective-permute-start.29 = (bf16[512,512]{1,0:T(8,128)(2,1)S(1)}, bf16[512,512]{1,0:T(8,128)(2,1)S(1)}, u32[]{:S(2)}, u32[]{:S(2)}) collective-permute-start(bf16[512,512]{1,0:T(8,128)(2,1)S(1)} %get-tuple-element.98), channel_id=1, source_target_pairs={{0,1},{1,0},{2,3},{3,2},{4,5},{5,4},{6,7},{7,6},{8,9},{9,8},{10,11... | collective-permute-start | bytes 1572872 | tf_op jit(solution)/shard_map/ppermute | solution.py:22
  124.8 14.8 %collective-permute-start.30 = (bf16[128,512]{1,0:T(8,128)(2,1)S(1)}, bf16[128,512]{1,0:T(8,128)(2,1)S(1)}, u32[]{:S(2)}, u32[]{:S(2)}) collective-permute-start(bf16[128,512]{1,0:T(8,128)(2,1)S(1)} %get-tuple-element.100), channel_id=1, source_target_pairs={{0,16},{16,32},{32,48},{48,0},{1,17},{17,33},{33,49},{49,1},{2,18}... | collective-permute-start | bytes 393224 | tf_op jit(solution)/shard_map/ppermute | solution.py:22
  126.2 13.5 %collective-permute-start.31 = (bf16[128,512]{1,0:T(8,128)(2,1)S(1)}, bf16[128,512]{1,0:T(8,128)(2,1)S(1)}, u32[]{:S(2)}, u32[]{:S(2)}) collective-permute-start(bf16[128,512]{1,0:T(8,128)(2,1)S(1)} %get-tuple-element.101), channel_id=1, source_target_pairs={{0,48},{16,0},{32,16},{48,32},{1,49},{17,1},{33,17},{49,33},{2,50}... | collective-permute-start | bytes 393224 | tf_op jit(solution)/shard_map/ppermute | solution.py:22
  129.0 11.5 %collective-permute-start.32 = (bf16[128,512]{1,0:T(8,128)(2,1)S(1)}, bf16[128,512]{1,0:T(8,128)(2,1)S(1)}, u32[]{:S(2)}, u32[]{:S(2)}) collective-permute-start(bf16[128,512]{1,0:T(8,128)(2,1)S(1)} %get-tuple-element.96), channel_id=1, source_target_pairs={{0,32},{16,48},{32,0},{48,16},{1,33},{17,49},{33,1},{49,17},{2,34}... | collective-permute-start | bytes 393224 | tf_op jit(solution)/shard_map/ppermute | solution.py:22
  (22 other events, 194.8 us)

commit v2 on v1

--- a/solution.py
+++ b/solution.py
@@ -382,7 +382,7 @@
     )
     got_l, got_r = send(g_left, "y", -1), send(g_right, "y", 1)
     left, right, z = weighed(near_body, (1, 2, 4), (x, x2, tie(b_left, d_zf), b_right), [block] * 3)
-    left, right, z = lax.optimization_barrier((left, right, z, got_l, got_r))[:3]
+    left, right = lax.optimization_barrier((left, right, got_l, got_r))[:2]
     sums = (send(left, "x", -1), send(right, "x", 1), send(z, "zl", 1))
     lifted, own_grad, to_other = weighed(
         functools.partial(back_body, rank),

time: 142 us -> 142 us (level)
  no operation moved by 1% of the time
where the time goes in v2:
time: 142 us
  waiting for transfers between devices  49.3 us (35%)
  starting transfers between devices  48.6 us (34%)
  Pallas kernels  35.1 us (25%)
  local copies, waits for them, and re-layouts  7.48 us (5%)
    ppermute x33, waiting for transfers between devices, send(): return lax.ppermute(a, axis, [(i, (i + step) % n) for i in range(n)])  49.3 us
    ppermute x33, starting transfers between devices, send(): return lax.ppermute(a, axis, [(i, (i + step) % n) for i in range(n)])  48.6 us
    pallas_call x6, Pallas kernels, with_weight(): pl.pallas_call(run, in_specs=[pl.BlockSpec(memory_space=pltpu.SMEM)] + [p...  26.3 us
    unnamed x42, local copies, waits for them, and re-layouts  7.36 us
    pallas_call x11, Pallas kernels, call(): pl.pallas_call(body, out_shape=out, in_specs=[pl.BlockSpec(memory_space=p...  7.08 us
  transfers between devices with their start and end apart: 33, of which 17 were waited for; matrix products, arithmetic and copies ran while one was open for 0% of the time, Pallas kernels for 24%

profile of v2, /device:TPU:32, one launch (start us, length us, event | category | flops | bytes accessed | tf_op | source)
XLA Modules:
  0.0 141.6 jit_solution(7345224275695650282)
XLA Ops:
  2.3 1.7 %collective-permute-start.5 = (bf16[512,512]{1,0:T(8,128)(2,1)}, bf16[512,512]{1,0:T(8,128)(2,1)S(1)}, u32[]{:S(2)}, u32[]{:S(2)}) collective-permute-start(bf16[512,512]{1,0:T(8,128)(2,1)} %dy_ref.7), channel_id=1, source_target_pairs={{0,12},{4,0},{8,4},{12,8},{1,13},{5,1},{9,5},{13,9},{2,14},{6,2},{... | collective-permute-start | bytes 1572872 | tf_op jit(solution)/shard_map/ppermute | solution.py:22
  5.9 3.3 %collective-permute-start.1 = (bf16[128,512]{1,0:T(8,128)(2,1)S(1)}, bf16[128,512]{1,0:T(8,128)(2,1)S(1)}, u32[]{:S(2)}, u32[]{:S(2)}) collective-permute-start(bf16[128,512]{1,0:T(8,128)(2,1)S(1)} %shard_map.170.own), channel_id=1, source_target_pairs={{0,16},{16,32},{32,48},{48,0},{1,17},{17,33},{33,49},{49,1},{2,18}... | collective-permute-start | bytes 393224 | tf_op jit(solution)/shard_map/ppermute | solution.py:22
  9.2 2.2 %collective-permute-start.2 = (bf16[128,512]{1,0:T(8,128)(2,1)S(1)}, bf16[128,512]{1,0:T(8,128)(2,1)S(1)}, u32[]{:S(2)}, u32[]{:S(2)}) collective-permute-start(bf16[128,512]{1,0:T(8,128)(2,1)S(1)} %shard_map.170.own), channel_id=1, source_target_pairs={{0,48},{16,0},{32,16},{48,32},{1,49},{17,1},{33,17},{49,33},{2,50}... | collective-permute-start | bytes 393224 | tf_op jit(solution)/shard_map/ppermute | solution.py:22
  11.5 4.9 %collective-permute-start.3 = (bf16[128,512]{1,0:T(8,128)(2,1)S(1)}, bf16[128,512]{1,0:T(8,128)(2,1)S(1)}, u32[]{:S(2)}, u32[]{:S(2)}) collective-permute-start(bf16[128,512]{1,0:T(8,128)(2,1)S(1)} %shard_map.170.own), channel_id=1, source_target_pairs={{0,32},{16,48},{32,0},{48,16},{1,33},{17,49},{33,1},{49,17},{2,34}... | collective-permute-start | bytes 393224 | tf_op jit(solution)/shard_map/ppermute | solution.py:22
  17.8 1.7 %shard_map.171.m_ref.refs_2_ = bf16[1024,512]{1,0:T(8,128)(2,1)S(1)} custom-call(s32[1,64]{1,0:T(1,128)S(1)} %bitcast.43, s32[1,64]{1,0:T(1,128)S(1)} %copy-done.20, s32[2]{0:T(128)S(1)} %pad_add_fusion.place_ref), custom_call_target="tpu_custom_call" | custom-call | bytes 2097152 | tf_op jit(solution)/shard_map/pallas_call | solution.py:78
  19.5 7.8 %collective-permute-done.3.far = bf16[128,512]{1,0:T(8,128)(2,1)S(1)} collective-permute-done((bf16[128,512]{1,0:T(8,128)(2,1)S(1)}, bf16[128,512]{1,0:T(8,128)(2,1)S(1)}, u32[]{:S(2)}, u32[]{:S(2)}) %collective-permute-start.3) | collective-permute-done | bytes 131104 | tf_op jit(solution)/shard_map/ppermute | solution.py:22
  32.0 1.7 %collective-permute-start.10 = (bf16[512,512]{1,0:T(8,128)(2,1)S(1)}, bf16[512,512]{1,0:T(8,128)(2,1)S(1)}, u32[]{:S(2)}, u32[]{:S(2)}) collective-permute-start(bf16[512,512]{1,0:T(8,128)(2,1)S(1)} %shard_map.172.own_ref.refs_4_), channel_id=1, source_target_pairs={{0,192},{64,0},{128,64},{192,128},{1,193},{65,1},{129,65},{193,129... | collective-permute-start | bytes 1572872 | tf_op jit(solution)/shard_map/ppermute | solution.py:22
  33.8 10.2 %collective-permute-done.6.v_ref = bf16[512,8192]{1,0:T(8,128)(2,1)} collective-permute-done((bf16[512,8192]{1,0:T(8,128)(2,1)}, bf16[512,8192]{1,0:T(8,128)(2,1)}, u32[]{:S(2)}, u32[]{:S(2)}) %collective-permute-start.6) | collective-permute-done | bytes 8388640 | tf_op jit(solution)/shard_map/ppermute | solution.py:22
  45.0 2.5 %shard_map.173 = bf16[512,512]{1,0:T(8,128)(2,1)S(1)} custom-call(s32[8]{0:T(128)S(1)} %stack.44.place_ref, bf16[512,8192]{1,0:T(8,128)(2,1)} %w_ref.11, bf16[512,8192]{1,0:T(8,128)(2,1)} %collective-permute-done.6.v_ref, bf16[512,512]{1,0:T(8,128)(2,1)S(1)} %copy-done, bf16[512,512]{1,0:T(8,128)(2,1)S(1)} %collective-permute-done.refs_1_), custom_call_target="tpu_custom_call" | custom-call | flops 536870912 | bytes 2621440 | tf_op jit(solution)/shard_map/pallas_call | solution.py:182
  49.3 3.0 %collective-permute-start.16 = (bf16[768,512]{1,0:T(8,128)(2,1)S(1)}, bf16[768,512]{1,0:T(8,128)(2,1)S(1)}, u32[]{:S(2)}, u32[]{:S(2)}) collective-permute-start(bf16[768,512]{1,0:T(8,128)(2,1)S(1)} %get-tuple-element.67), channel_id=1, source_target_pairs={{0,12},{4,0},{8,4},{12,8},{1,13},{5,1},{9,5},{13,9},{2,14},{6,2},{... | collective-permute-start | bytes 2359304 | tf_op jit(solution)/shard_map/ppermute | solution.py:22
  53.8 2.1 %collective-permute-start.11 = (bf16[256,512]{1,0:T(8,128)(2,1)S(1)}, bf16[256,512]{1,0:T(8,128)(2,1)S(1)}, u32[]{:S(2)}, u32[]{:S(2)}) collective-permute-start(bf16[256,512]{1,0:T(8,128)(2,1)S(1)} %slice.9), channel_id=1, source_target_pairs={{0,192},{64,0},{128,64},{192,128},{1,193},{65,1},{129,65},{193,129... | collective-permute-start | bytes 786440 | tf_op jit(solution)/shard_map/ppermute | solution.py:22
  55.9 5.3 %collective-permute-done.9.far_d_ref.refs_7_ = bf16[256,512]{1,0:T(8,128)(2,1)S(1)} collective-permute-done((bf16[256,512]{1,0:T(8,128)(2,1)S(1)}, bf16[256,512]{1,0:T(8,128)(2,1)S(1)}, u32[]{:S(2)}, u32[]{:S(2)}) %collective-permute-start.9) | collective-permute-done | bytes 262176 | tf_op jit(solution)/shard_map/ppermute | solution.py:22
  61.6 4.1 %shard_map.174 = (bf16[768,512]{1,0:T(8,128)(2,1)S(1)}, bf16[768,512]{1,0:T(8,128)(2,1)S(1)}) custom-call(s32[8]{0:T(128)S(1)} %stack.44.place_ref, bf16[512,8192]{1,0:T(8,128)(2,1)} %w_ref.11, bf16[512,8192]{1,0:T(8,128)(2,1)} %collective-permute-done.6.v_ref, bf16[512,512]{1,0:T(8,128)(2,1)S(1)} %copy-done, ...), custom_call_target="tpu_custom_call" | custom-call | flops 1610612736 | bytes 6291456 | tf_op jit(solution)/shard_map/pallas_call | solution.py:182
  68.4 1.8 %collective-permute-start.15 = (f32[32,512]{1,0:T(8,128)S(1)}, f32[32,512]{1,0:T(8,128)S(1)}, u32[]{:S(2)}, u32[]{:S(2)}) collective-permute-start(f32[32,512]{1,0:T(8,128)S(1)} %add.133), channel_id=1, source_target_pairs={{0,2},{2,0},{1,3},{3,1},{4,6},{6,4},{5,7},{7,5},{8,10},{10,8},{9,1... | collective-permute-start | bytes 196616 | tf_op jit(solution)/shard_map/ppermute | solution.py:22
  70.2 2.6 %collective-permute-done.15 = f32[32,512]{1,0:T(8,128)S(1)} collective-permute-done((f32[32,512]{1,0:T(8,128)S(1)}, f32[32,512]{1,0:T(8,128)S(1)}, u32[]{:S(2)}, u32[]{:S(2)}) %collective-permute-start.15) | collective-permute-done | bytes 65568 | tf_op jit(solution)/shard_map/ppermute | solution.py:22
  73.1 5.6 %shard_map.177 = (f32[512,512]{1,0:T(8,128)S(1)}, f32[512,512]{1,0:T(8,128)S(1)}) custom-call(s32[8]{0:T(128)S(1)} %stack.44.place_ref, bf16[512,8192]{1,0:T(8,128)(2,1)} %w_ref.11, bf16[512,8192]{1,0:T(8,128)(2,1)} %collective-permute-done.6.v_ref, bf16[512,512]{1,0:T(8,128)(2,1)S(1)} %copy-done.2, bf16[512,512]{1,0:T(8,128)(2,1)S(1)} %copy-done.4, ...), custom_call_target="tpu_custom_call" | custom-call | flops 2147483648 | bytes 8388608 | tf_op jit(solution)/shard_map/pallas_call | solution.py:182
  78.7 2.8 %collective-permute-start.18 = (f32[32,512]{1,0:T(8,128)S(1)}, f32[32,512]{1,0:T(8,128)S(1)}, u32[]{:S(2)}, u32[]{:S(2)}) collective-permute-start(f32[32,512]{1,0:T(8,128)S(1)} %add.135), channel_id=1, source_target_pairs={{0,8},{4,12},{8,0},{12,4},{1,9},{5,13},{9,1},{13,5},{2,10},{6,14},... | collective-permute-start | bytes 196616 | tf_op jit(solution)/shard_map/ppermute | solution.py:22
  81.6 4.3 %shard_map.179 = (f32[512,512]{1,0:T(8,128)S(1)}, f32[512,512]{1,0:T(8,128)S(1)}) custom-call(s32[8]{0:T(128)S(1)} %stack.44.place_ref, bf16[512,8192]{1,0:T(8,128)(2,1)} %w_ref.11, bf16[512,8192]{1,0:T(8,128)(2,1)} %collective-permute-done.6.v_ref, bf16[512,512]{1,0:T(8,128)(2,1)S(1)} %shard_map.178.refs_0_, ...), custom_call_target="tpu_custom_call" | custom-call | flops 1610612736 | bytes 9437184 | tf_op jit(solution)/shard_map/pallas_call | solution.py:182
  87.1 2.1 %collective-permute-start.21 = (bf16[768,512]{1,0:T(8,128)(2,1)S(1)}, bf16[768,512]{1,0:T(8,128)(2,1)S(1)}, u32[]{:S(2)}, u32[]{:S(2)}) collective-permute-start(bf16[768,512]{1,0:T(8,128)(2,1)S(1)} %get-tuple-element.80), channel_id=1, source_target_pairs={{0,12},{4,0},{8,4},{12,8},{1,13},{5,1},{9,5},{13,9},{2,14},{6,2},{... | collective-permute-start | bytes 2359304 | tf_op jit(solution)/shard_map/ppermute | solution.py:22
  89.7 1.6 %collective-permute-start.22 = (bf16[256,512]{1,0:T(8,128)(2,1)S(1)}, bf16[256,512]{1,0:T(8,128)(2,1)S(1)}, u32[]{:S(2)}, u32[]{:S(2)}) collective-permute-start(bf16[256,512]{1,0:T(8,128)(2,1)S(1)} %get-tuple-element.83), channel_id=1, source_target_pairs={{0,64},{64,128},{128,192},{192,0},{1,65},{65,129},{129,193},{193,1... | collective-permute-start | bytes 786440 | tf_op jit(solution)/shard_map/ppermute | solution.py:22
  91.3 1.7 %collective-permute-start.23 = (bf16[256,512]{1,0:T(8,128)(2,1)S(1)}, bf16[256,512]{1,0:T(8,128)(2,1)S(1)}, u32[]{:S(2)}, u32[]{:S(2)}) collective-permute-start(bf16[256,512]{1,0:T(8,128)(2,1)S(1)} %get-tuple-element.84), channel_id=1, source_target_pairs={{0,192},{64,0},{128,64},{192,128},{1,193},{65,1},{129,65},{193,129... | collective-permute-start | bytes 786440 | tf_op jit(solution)/shard_map/ppermute | solution.py:22
  93.5 3.8 %collective-permute-done.22.got_down_ref = bf16[256,512]{1,0:T(8,128)(2,1)S(1)} collective-permute-done((bf16[256,512]{1,0:T(8,128)(2,1)S(1)}, bf16[256,512]{1,0:T(8,128)(2,1)S(1)}, u32[]{:S(2)}, u32[]{:S(2)}) %collective-permute-start.22) | collective-permute-done | bytes 262176 | tf_op jit(solution)/shard_map/ppermute | solution.py:22
  98.4 3.0 %collective-permute-start.24 = (bf16[512,512]{1,0:T(8,128)(2,1)S(1)}, bf16[512,512]{1,0:T(8,128)(2,1)S(1)}, u32[]{:S(2)}, u32[]{:S(2)}) collective-permute-start(bf16[512,512]{1,0:T(8,128)(2,1)S(1)} %get-tuple-element.85), channel_id=1, source_target_pairs={{0,192},{64,0},{128,64},{192,128},{1,193},{65,1},{129,65},{193,129... | collective-permute-start | bytes 1572872 | tf_op jit(solution)/shard_map/ppermute | solution.py:22
  101.4 2.9 %collective-permute-done.20.refs_9_ = bf16[512,512]{1,0:T(8,128)(2,1)S(1)} collective-permute-done((bf16[512,512]{1,0:T(8,128)(2,1)S(1)}, bf16[512,512]{1,0:T(8,128)(2,1)S(1)}, u32[]{:S(2)}, u32[]{:S(2)}) %collective-permute-start.20) | collective-permute-done | bytes 524320 | tf_op jit(solution)/shard_map/ppermute | solution.py:22
  105.1 4.2 %shard_map.180 = (bf16[512,512]{1,0:T(8,128)(2,1)S(1)}, bf16[512,512]{1,0:T(8,128)(2,1)S(1)}, bf16[512,512]{1,0:T(8,128)(2,1)S(1)}) custom-call(s32[8]{0:T(128)S(1)} %stack.44.place_ref, bf16[512,8192]{1,0:T(8,128)(2,1)} %w_ref.11, bf16[512,8192]{1,0:T(8,128)(2,1)} %collective-permute-done.6.v_ref, bf16[512,512]{1,0:T(8,128)(2,1)S(1)} %copy-done.1, ...), custom_call_target="tpu_custom_call" | custom-call | flops 1610612736 | bytes 7340032 | tf_op jit(solution)/shard_map/pallas_call | solution.py:182
  109.6 3.4 %collective-permute-done.25.b_ref = bf16[512,512]{1,0:T(8,128)(2,1)S(1)} collective-permute-done((bf16[512,512]{1,0:T(8,128)(2,1)S(1)}, bf16[512,512]{1,0:T(8,128)(2,1)S(1)}, u32[]{:S(2)}, u32[]{:S(2)}) %collective-permute-start.25) | collective-permute-done | bytes 524320 | tf_op jit(solution)/shard_map/ppermute | solution.py:22
  113.3 1.7 %collective-permute-start.27 = (bf16[512,512]{1,0:T(8,128)(2,1)S(1)}, bf16[512,512]{1,0:T(8,128)(2,1)S(1)}, u32[]{:S(2)}, u32[]{:S(2)}) collective-permute-start(bf16[512,512]{1,0:T(8,128)(2,1)S(1)} %get-tuple-element.88), channel_id=1, source_target_pairs={{0,4},{4,8},{8,12},{12,0},{1,5},{5,9},{9,13},{13,1},{2,6},{6,10},{... | collective-permute-start | bytes 1572872 | tf_op jit(solution)/shard_map/ppermute | solution.py:22
  115.8 5.7 %shard_map.183 = (f32[512,512]{1,0:T(8,128)S(1)}, f32[512,512]{1,0:T(8,128)S(1)}, bf16[512,512]{1,0:T(8,128)(2,1)S(1)}) custom-call(s32[8]{0:T(128)S(1)} %stack.44.place_ref, bf16[512,8192]{1,0:T(8,128)(2,1)} %w_ref.11, bf16[512,8192]{1,0:T(8,128)(2,1)} %collective-permute-done.6.v_ref, bf16[512,512]{1,0:T(8,128)(2,1)S(1)} %copy-done.1, ...), custom_call_target="tpu_custom_call" | custom-call | flops 1073741824 | bytes 11599872 | tf_op jit(solution)/shard_map/pallas_call | solution.py:182
  122.5 1.8 %collective-permute-done.27.b = bf16[512,512]{1,0:T(8,128)(2,1)S(1)} collective-permute-done((bf16[512,512]{1,0:T(8,128)(2,1)S(1)}, bf16[512,512]{1,0:T(8,128)(2,1)S(1)}, u32[]{:S(2)}, u32[]{:S(2)}) %collective-permute-start.27) | collective-permute-done | bytes 524320 | tf_op jit(solution)/shard_map/ppermute | solution.py:22
  126.2 2.9 %collective-permute-start.31 = (bf16[128,512]{1,0:T(8,128)(2,1)S(1)}, bf16[128,512]{1,0:T(8,128)(2,1)S(1)}, u32[]{:S(2)}, u32[]{:S(2)}) collective-permute-start(bf16[128,512]{1,0:T(8,128)(2,1)S(1)} %get-tuple-element.99), channel_id=1, source_target_pairs={{0,48},{16,0},{32,16},{48,32},{1,49},{17,1},{33,17},{49,33},{2,50}... | collective-permute-start | bytes 393224 | tf_op jit(solution)/shard_map/ppermute | solution.py:22
  129.0 2.2 %collective-permute-start.32 = (bf16[128,512]{1,0:T(8,128)(2,1)S(1)}, bf16[128,512]{1,0:T(8,128)(2,1)S(1)}, u32[]{:S(2)}, u32[]{:S(2)}) collective-permute-start(bf16[128,512]{1,0:T(8,128)(2,1)S(1)} %get-tuple-element.94), channel_id=1, source_target_pairs={{0,32},{16,48},{32,0},{48,16},{1,33},{17,49},{33,1},{49,17},{2,34}... | collective-permute-start | bytes 393224 | tf_op jit(solution)/shard_map/ppermute | solution.py:22
  133.1 6.5 %collective-permute-done.30.refs_1_ = bf16[128,512]{1,0:T(8,128)(2,1)S(1)} collective-permute-done((bf16[128,512]{1,0:T(8,128)(2,1)S(1)}, bf16[128,512]{1,0:T(8,128)(2,1)S(1)}, u32[]{:S(2)}, u32[]{:S(2)}) %collective-permute-start.30) | collective-permute-done | bytes 131104 | tf_op jit(solution)/shard_map/ppermute | solution.py:22
  (102 shorter events, 29.5 us)
Async XLA Ops:
  0.6 5.2 %collective-permute-start = (bf16[512,512]{1,0:T(8,128)(2,1)}, bf16[512,512]{1,0:T(8,128)(2,1)S(1)}, u32[]{:S(2)}, u32[]{:S(2)}) collective-permute-start(bf16[512,512]{1,0:T(8,128)(2,1)} %x_ref.7), channel_id=1, source_target_pairs={{0,1},{1,0},{2,3},{3,2},{4,5},{5,4},{6,7},{7,6},{8,9},{9,8},{10,11... | collective-permute-start | bytes 1572872 | tf_op jit(solution)/shard_map/ppermute | solution.py:22
  0.7 28.1 %collective-permute-start.4 = (bf16[512,512]{1,0:T(8,128)(2,1)}, bf16[512,512]{1,0:T(8,128)(2,1)S(1)}, u32[]{:S(2)}, u32[]{:S(2)}) collective-permute-start(bf16[512,512]{1,0:T(8,128)(2,1)} %dy_ref.7), channel_id=1, source_target_pairs={{0,4},{4,8},{8,12},{12,0},{1,5},{5,9},{9,13},{13,1},{2,6},{6,10},{... | collective-permute-start | bytes 1572872 | tf_op jit(solution)/shard_map/ppermute | solution.py:22
  2.3 27.3 %collective-permute-start.5 = (bf16[512,512]{1,0:T(8,128)(2,1)}, bf16[512,512]{1,0:T(8,128)(2,1)S(1)}, u32[]{:S(2)}, u32[]{:S(2)}) collective-permute-start(bf16[512,512]{1,0:T(8,128)(2,1)} %dy_ref.7), channel_id=1, source_target_pairs={{0,12},{4,0},{8,4},{12,8},{1,13},{5,1},{9,5},{13,9},{2,14},{6,2},{... | collective-permute-start | bytes 1572872 | tf_op jit(solution)/shard_map/ppermute | solution.py:22
  5.9 13.6 %collective-permute-start.1 = (bf16[128,512]{1,0:T(8,128)(2,1)S(1)}, bf16[128,512]{1,0:T(8,128)(2,1)S(1)}, u32[]{:S(2)}, u32[]{:S(2)}) collective-permute-start(bf16[128,512]{1,0:T(8,128)(2,1)S(1)} %shard_map.170.own), channel_id=1, source_target_pairs={{0,16},{16,32},{32,48},{48,0},{1,17},{17,33},{33,49},{49,1},{2,18}... | collective-permute-start | bytes 393224 | tf_op jit(solution)/shard_map/ppermute | solution.py:22
  9.2 10.2 %collective-permute-start.2 = (bf16[128,512]{1,0:T(8,128)(2,1)S(1)}, bf16[128,512]{1,0:T(8,128)(2,1)S(1)}, u32[]{:S(2)}, u32[]{:S(2)}) collective-permute-start(bf16[128,512]{1,0:T(8,128)(2,1)S(1)} %shard_map.170.own), channel_id=1, source_target_pairs={{0,48},{16,0},{32,16},{48,32},{1,49},{17,1},{33,17},{49,33},{2,50}... | collective-permute-start | bytes 393224 | tf_op jit(solution)/shard_map/ppermute | solution.py:22
  11.5 15.8 %collective-permute-start.3 = (bf16[128,512]{1,0:T(8,128)(2,1)S(1)}, bf16[128,512]{1,0:T(8,128)(2,1)S(1)}, u32[]{:S(2)}, u32[]{:S(2)}) collective-permute-start(bf16[128,512]{1,0:T(8,128)(2,1)S(1)} %shard_map.170.own), channel_id=1, source_target_pairs={{0,32},{16,48},{32,0},{48,16},{1,33},{17,49},{33,1},{49,17},{2,34}... | collective-permute-start | bytes 393224 | tf_op jit(solution)/shard_map/ppermute | solution.py:22
  30.4 13.5 %collective-permute-start.6 = (bf16[512,8192]{1,0:T(8,128)(2,1)}, bf16[512,8192]{1,0:T(8,128)(2,1)}, u32[]{:S(2)}, u32[]{:S(2)}) collective-permute-start(bf16[512,8192]{1,0:T(8,128)(2,1)} %w_ref.11), channel_id=1, source_target_pairs={{0,1},{1,0},{2,3},{3,2},{4,5},{5,4},{6,7},{7,6},{8,9},{9,8},{10,11... | collective-permute-start | bytes 25165832 | tf_op jit(solution)/shard_map/ppermute | solution.py:22
  30.4 17.1 %collective-permute-start.8 = (bf16[512,512]{1,0:T(8,128)(2,1)S(1)}, bf16[512,512]{1,0:T(8,128)(2,1)S(1)}, u32[]{:S(2)}, u32[]{:S(2)}) collective-permute-start(bf16[512,512]{1,0:T(8,128)(2,1)S(1)} %shard_map.172.own_ref.refs_4_), channel_id=1, source_target_pairs={{0,64},{64,128},{128,192},{192,0},{1,65},{65,129},{129,193},{193,1... | collective-permute-start | bytes 1572872 | tf_op jit(solution)/shard_map/ppermute | solution.py:22
  32.0 15.6 %collective-permute-start.10 = (bf16[512,512]{1,0:T(8,128)(2,1)S(1)}, bf16[512,512]{1,0:T(8,128)(2,1)S(1)}, u32[]{:S(2)}, u32[]{:S(2)}) collective-permute-start(bf16[512,512]{1,0:T(8,128)(2,1)S(1)} %shard_map.172.own_ref.refs_4_), channel_id=1, source_target_pairs={{0,192},{64,0},{128,64},{192,128},{1,193},{65,1},{129,65},{193,129... | collective-permute-start | bytes 1572872 | tf_op jit(solution)/shard_map/ppermute | solution.py:22
  33.7 14.2 %collective-permute-start.12 = (bf16[512,512]{1,0:T(8,128)(2,1)}, bf16[512,512]{1,0:T(8,128)(2,1)}, u32[]{:S(2)}, u32[]{:S(2)}) collective-permute-start(bf16[512,512]{1,0:T(8,128)(2,1)} %dy_ref.7), channel_id=1, source_target_pairs={{0,2},{2,0},{1,3},{3,1},{4,6},{6,4},{5,7},{7,5},{8,10},{10,8},{9,1... | collective-permute-start | bytes 1572872 | tf_op jit(solution)/shard_map/ppermute | solution.py:22
  47.5 14.1 %collective-permute-start.7 = (bf16[512,512]{1,0:T(8,128)(2,1)S(1)}, bf16[512,512]{1,0:T(8,128)(2,1)S(1)}, u32[]{:S(2)}, u32[]{:S(2)}) collective-permute-start(bf16[512,512]{1,0:T(8,128)(2,1)S(1)} %shard_map.173), channel_id=1, source_target_pairs={{0,2},{2,0},{1,3},{3,1},{4,6},{6,4},{5,7},{7,5},{8,10},{10,8},{9,1... | collective-permute-start | bytes 1572872 | tf_op jit(solution)/shard_map/ppermute | solution.py:22
  49.0 23.7 %collective-permute-start.13 = (bf16[768,512]{1,0:T(8,128)(2,1)S(1)}, bf16[768,512]{1,0:T(8,128)(2,1)S(1)}, u32[]{:S(2)}, u32[]{:S(2)}) collective-permute-start(bf16[768,512]{1,0:T(8,128)(2,1)S(1)} %get-tuple-element.65), channel_id=1, source_target_pairs={{0,4},{4,8},{8,12},{12,0},{1,5},{5,9},{9,13},{13,1},{2,6},{6,10},{... | collective-permute-start | bytes 2359304 | tf_op jit(solution)/shard_map/ppermute | solution.py:22
  49.3 23.4 %collective-permute-start.16 = (bf16[768,512]{1,0:T(8,128)(2,1)S(1)}, bf16[768,512]{1,0:T(8,128)(2,1)S(1)}, u32[]{:S(2)}, u32[]{:S(2)}) collective-permute-start(bf16[768,512]{1,0:T(8,128)(2,1)S(1)} %get-tuple-element.67), channel_id=1, source_target_pairs={{0,12},{4,0},{8,4},{12,8},{1,13},{5,1},{9,5},{13,9},{2,14},{6,2},{... | collective-permute-start | bytes 2359304 | tf_op jit(solution)/shard_map/ppermute | solution.py:22
  52.3 8.9 %collective-permute-start.9 = (bf16[256,512]{1,0:T(8,128)(2,1)S(1)}, bf16[256,512]{1,0:T(8,128)(2,1)S(1)}, u32[]{:S(2)}, u32[]{:S(2)}) collective-permute-start(bf16[256,512]{1,0:T(8,128)(2,1)S(1)} %slice.8), channel_id=1, source_target_pairs={{0,64},{64,128},{128,192},{192,0},{1,65},{65,129},{129,193},{193,1... | collective-permute-start | bytes 786440 | tf_op jit(solution)/shard_map/ppermute | solution.py:22
  53.8 7.8 %collective-permute-start.11 = (bf16[256,512]{1,0:T(8,128)(2,1)S(1)}, bf16[256,512]{1,0:T(8,128)(2,1)S(1)}, u32[]{:S(2)}, u32[]{:S(2)}) collective-permute-start(bf16[256,512]{1,0:T(8,128)(2,1)S(1)} %slice.9), channel_id=1, source_target_pairs={{0,192},{64,0},{128,64},{192,128},{1,193},{65,1},{129,65},{193,129... | collective-permute-start | bytes 786440 | tf_op jit(solution)/shard_map/ppermute | solution.py:22
  68.4 4.4 %collective-permute-start.15 = (f32[32,512]{1,0:T(8,128)S(1)}, f32[32,512]{1,0:T(8,128)S(1)}, u32[]{:S(2)}, u32[]{:S(2)}) collective-permute-start(f32[32,512]{1,0:T(8,128)S(1)} %add.133), channel_id=1, source_target_pairs={{0,2},{2,0},{1,3},{3,1},{4,6},{6,4},{5,7},{7,5},{8,10},{10,8},{9,1... | collective-permute-start | bytes 196616 | tf_op jit(solution)/shard_map/ppermute | solution.py:22
  72.7 5.9 %collective-permute-start.17 = (f32[32,512]{1,0:T(8,128)S(1)}, f32[32,512]{1,0:T(8,128)S(1)}, u32[]{:S(2)}, u32[]{:S(2)}) collective-permute-start(f32[32,512]{1,0:T(8,128)S(1)} %add.134), channel_id=1, source_target_pairs={{0,4},{4,8},{8,12},{12,0},{1,5},{5,9},{9,13},{13,1},{2,6},{6,10},{... | collective-permute-start | bytes 196616 | tf_op jit(solution)/shard_map/ppermute | solution.py:22
  78.7 7.2 %collective-permute-start.18 = (f32[32,512]{1,0:T(8,128)S(1)}, f32[32,512]{1,0:T(8,128)S(1)}, u32[]{:S(2)}, u32[]{:S(2)}) collective-permute-start(f32[32,512]{1,0:T(8,128)S(1)} %add.135), channel_id=1, source_target_pairs={{0,8},{4,12},{8,0},{12,4},{1,9},{5,13},{9,1},{13,5},{2,10},{6,14},... | collective-permute-start | bytes 196616 | tf_op jit(solution)/shard_map/ppermute | solution.py:22
  85.9 19.2 %collective-permute-start.19 = (bf16[768,512]{1,0:T(8,128)(2,1)S(1)}, bf16[768,512]{1,0:T(8,128)(2,1)S(1)}, u32[]{:S(2)}, u32[]{:S(2)}) collective-permute-start(bf16[768,512]{1,0:T(8,128)(2,1)S(1)} %get-tuple-element.77), channel_id=1, source_target_pairs={{0,4},{4,8},{8,12},{12,0},{1,5},{5,9},{9,13},{13,1},{2,6},{6,10},{... | collective-permute-start | bytes 2359304 | tf_op jit(solution)/shard_map/ppermute | solution.py:22
  87.1 18.0 %collective-permute-start.21 = (bf16[768,512]{1,0:T(8,128)(2,1)S(1)}, bf16[768,512]{1,0:T(8,128)(2,1)S(1)}, u32[]{:S(2)}, u32[]{:S(2)}) collective-permute-start(bf16[768,512]{1,0:T(8,128)(2,1)S(1)} %get-tuple-element.80), channel_id=1, source_target_pairs={{0,12},{4,0},{8,4},{12,8},{1,13},{5,1},{9,5},{13,9},{2,14},{6,2},{... | collective-permute-start | bytes 2359304 | tf_op jit(solution)/shard_map/ppermute | solution.py:22
  89.7 7.7 %collective-permute-start.22 = (bf16[256,512]{1,0:T(8,128)(2,1)S(1)}, bf16[256,512]{1,0:T(8,128)(2,1)S(1)}, u32[]{:S(2)}, u32[]{:S(2)}) collective-permute-start(bf16[256,512]{1,0:T(8,128)(2,1)S(1)} %get-tuple-element.83), channel_id=1, source_target_pairs={{0,64},{64,128},{128,192},{192,0},{1,65},{65,129},{129,193},{193,1... | collective-permute-start | bytes 786440 | tf_op jit(solution)/shard_map/ppermute | solution.py:22
  91.3 6.4 %collective-permute-start.23 = (bf16[256,512]{1,0:T(8,128)(2,1)S(1)}, bf16[256,512]{1,0:T(8,128)(2,1)S(1)}, u32[]{:S(2)}, u32[]{:S(2)}) collective-permute-start(bf16[256,512]{1,0:T(8,128)(2,1)S(1)} %get-tuple-element.84), channel_id=1, source_target_pairs={{0,192},{64,0},{128,64},{192,128},{1,193},{65,1},{129,65},{193,129... | collective-permute-start | bytes 786440 | tf_op jit(solution)/shard_map/ppermute | solution.py:22
  93.0 11.3 %collective-permute-start.20 = (bf16[512,512]{1,0:T(8,128)(2,1)S(1)}, bf16[512,512]{1,0:T(8,128)(2,1)S(1)}, u32[]{:S(2)}, u32[]{:S(2)}) collective-permute-start(bf16[512,512]{1,0:T(8,128)(2,1)S(1)} %shard_map.178.refs_0_), channel_id=1, source_target_pairs={{0,2},{2,0},{1,3},{3,1},{4,6},{6,4},{5,7},{7,5},{8,10},{10,8},{9,1... | collective-permute-start | bytes 1572872 | tf_op jit(solution)/shard_map/ppermute | solution.py:22
  98.4 11.2 %collective-permute-start.24 = (bf16[512,512]{1,0:T(8,128)(2,1)S(1)}, bf16[512,512]{1,0:T(8,128)(2,1)S(1)}, u32[]{:S(2)}, u32[]{:S(2)}) collective-permute-start(bf16[512,512]{1,0:T(8,128)(2,1)S(1)} %get-tuple-element.85), channel_id=1, source_target_pairs={{0,192},{64,0},{128,64},{192,128},{1,193},{65,1},{129,65},{193,129... | collective-permute-start | bytes 1572872 | tf_op jit(solution)/shard_map/ppermute | solution.py:22
  101.4 11.7 %collective-permute-start.25 = (bf16[512,512]{1,0:T(8,128)(2,1)S(1)}, bf16[512,512]{1,0:T(8,128)(2,1)S(1)}, u32[]{:S(2)}, u32[]{:S(2)}) collective-permute-start(bf16[512,512]{1,0:T(8,128)(2,1)S(1)} %get-tuple-element.86), channel_id=1, source_target_pairs={{0,64},{64,128},{128,192},{192,0},{1,65},{65,129},{129,193},{193,1... | collective-permute-start | bytes 1572872 | tf_op jit(solution)/shard_map/ppermute | solution.py:22
  113.0 9.5 %collective-permute-start.26 = (bf16[512,512]{1,0:T(8,128)(2,1)S(1)}, bf16[512,512]{1,0:T(8,128)(2,1)S(1)}, u32[]{:S(2)}, u32[]{:S(2)}) collective-permute-start(bf16[512,512]{1,0:T(8,128)(2,1)S(1)} %get-tuple-element.87), channel_id=1, source_target_pairs={{0,12},{4,0},{8,4},{12,8},{1,13},{5,1},{9,5},{13,9},{2,14},{6,2},{... | collective-permute-start | bytes 1572872 | tf_op jit(solution)/shard_map/ppermute | solution.py:22
  113.3 11.0 %collective-permute-start.27 = (bf16[512,512]{1,0:T(8,128)(2,1)S(1)}, bf16[512,512]{1,0:T(8,128)(2,1)S(1)}, u32[]{:S(2)}, u32[]{:S(2)}) collective-permute-start(bf16[512,512]{1,0:T(8,128)(2,1)S(1)} %get-tuple-element.88), channel_id=1, source_target_pairs={{0,4},{4,8},{8,12},{12,0},{1,5},{5,9},{9,13},{13,1},{2,6},{6,10},{... | collective-permute-start | bytes 1572872 | tf_op jit(solution)/shard_map/ppermute | solution.py:22
  115.0 9.3 %collective-permute-start.28 = (bf16[512,512]{1,0:T(8,128)(2,1)S(1)}, bf16[512,512]{1,0:T(8,128)(2,1)S(1)}, u32[]{:S(2)}, u32[]{:S(2)}) collective-permute-start(bf16[512,512]{1,0:T(8,128)(2,1)S(1)} %get-tuple-element.89), channel_id=1, source_target_pairs={{0,2},{2,0},{1,3},{3,1},{4,6},{6,4},{5,7},{7,5},{8,10},{10,8},{9,1... | collective-permute-start | bytes 1572872 | tf_op jit(solution)/shard_map/ppermute | solution.py:22
  121.6 10.6 %collective-permute-start.29 = (bf16[512,512]{1,0:T(8,128)(2,1)S(1)}, bf16[512,512]{1,0:T(8,128)(2,1)S(1)}, u32[]{:S(2)}, u32[]{:S(2)}) collective-permute-start(bf16[512,512]{1,0:T(8,128)(2,1)S(1)} %get-tuple-element.96), channel_id=1, source_target_pairs={{0,1},{1,0},{2,3},{3,2},{4,5},{5,4},{6,7},{7,6},{8,9},{9,8},{10,11... | collective-permute-start | bytes 1572872 | tf_op jit(solution)/shard_map/ppermute | solution.py:22
  124.8 14.8 %collective-permute-start.30 = (bf16[128,512]{1,0:T(8,128)(2,1)S(1)}, bf16[128,512]{1,0:T(8,128)(2,1)S(1)}, u32[]{:S(2)}, u32[]{:S(2)}) collective-permute-start(bf16[128,512]{1,0:T(8,128)(2,1)S(1)} %get-tuple-element.98), channel_id=1, source_target_pairs={{0,16},{16,32},{32,48},{48,0},{1,17},{17,33},{33,49},{49,1},{2,18}... | collective-permute-start | bytes 393224 | tf_op jit(solution)/shard_map/ppermute | solution.py:22
  126.2 13.5 %collective-permute-start.31 = (bf16[128,512]{1,0:T(8,128)(2,1)S(1)}, bf16[128,512]{1,0:T(8,128)(2,1)S(1)}, u32[]{:S(2)}, u32[]{:S(2)}) collective-permute-start(bf16[128,512]{1,0:T(8,128)(2,1)S(1)} %get-tuple-element.99), channel_id=1, source_target_pairs={{0,48},{16,0},{32,16},{48,32},{1,49},{17,1},{33,17},{49,33},{2,50}... | collective-permute-start | bytes 393224 | tf_op jit(solution)/shard_map/ppermute | solution.py:22
  129.0 11.5 %collective-permute-start.32 = (bf16[128,512]{1,0:T(8,128)(2,1)S(1)}, bf16[128,512]{1,0:T(8,128)(2,1)S(1)}, u32[]{:S(2)}, u32[]{:S(2)}) collective-permute-start(bf16[128,512]{1,0:T(8,128)(2,1)S(1)} %get-tuple-element.94), channel_id=1, source_target_pairs={{0,32},{16,48},{32,0},{48,16},{1,33},{17,49},{33,1},{49,17},{2,34}... | collective-permute-start | bytes 393224 | tf_op jit(solution)/shard_map/ppermute | solution.py:22
  (22 other events, 194.8 us)
